TPU v7x, 512 devices: a whole 4x4x16 slice. The times are simulated.
512 devices in a mesh: comm: 8 (over y, core), node: 64 (over z, x).
Axes of the slice: x: 4, y: 4, z: 16, core: 2. Of those that a mesh axis runs over, the one named last changes fastest.
Arguments:
- embeddings: float32 [131072, 128], P('node'), may hold values from -1.2 to 75
- prototypes: float32 [4096, 128], P('comm'), may hold values from -3.6 to 3.6
- plan_grad: bfloat16 [131072, 4096], P('node', 'comm'), may hold values from -3 to 3
Outputs:
- grad_emb: float32 [131072, 128], P(('node', 'comm'))
- grad_proto: float32 [4096, 128], P(('comm', 'node'))
All inputs are finite; a program needn't handle non-finite values.
Results may differ from a plain program's by a relative error of at most 0.0022.
Values sent between devices are 32-bit elements; how exact they have to be, the bound alone decides.
No kernel may reach another device: no remote copies, remote signals or barrier semaphores. Data moves between devices by JAX's collectives and lax.ppermute only.
A program may use at most 64 MiB of HBM per device.

v0:
```python
import math

import jax
import jax.numpy as jnp
from jax import lax
from jax.sharding import PartitionSpec as P

INV_EPS = 20.0


def row_lse(shifted):
    peak = lax.pmax(jnp.max(shifted, axis=1), "comm")
    mass = lax.psum(jnp.sum(jnp.exp(shifted - peak[:, None]), axis=1), "comm")
    return peak + jnp.log(mass)


def col_lse(shifted):
    peak = lax.pmax(jnp.max(shifted, axis=0), "node")
    mass = lax.psum(jnp.sum(jnp.exp(shifted - peak[None, :]), axis=0), "node")
    return peak + jnp.log(mass)


def row_total(values):
    return lax.psum(values, "comm")


def col_total(values):
    return lax.psum(values, "node")


def on_device(embeddings, prototypes, plan_grad):
    rows = embeddings.shape[0]
    local = prototypes.shape[0]
    comm_count = lax.axis_size("comm")
    node_count = lax.axis_size("node")
    log_mass = math.log(rows * node_count / (local * comm_count))
    factor = local * comm_count / (rows * node_count)
    logits = (
        jnp.dot(
            embeddings,
            prototypes.T,
            precision=lax.Precision.HIGHEST,
            preferred_element_type=jnp.float32,
        )
        * INV_EPS
    )
    f1 = -row_lse(logits)
    g1 = log_mass - col_lse(logits + f1[:, None])
    f2 = -row_lse(logits + g1[None, :])
    g2 = log_mass - col_lse(logits + f2[:, None])
    plan = jnp.exp(logits + f2[:, None] + g2[None, :])
    weighted = plan_grad.astype(jnp.float32) * plan
    dg2 = col_total(jnp.sum(weighted, axis=0))
    df2 = row_total(jnp.sum(weighted, axis=1) - factor * jnp.sum(plan * dg2[None, :], axis=1))
    second = jnp.exp(logits + f2[:, None] + g1[None, :])
    dg1 = -col_total(jnp.sum(second * df2[:, None], axis=0))
    first = jnp.exp(logits + f1[:, None])
    scaled = jnp.exp(logits + f1[:, None] + (g1 - log_mass)[None, :])
    df1 = -row_total(jnp.sum(scaled * dg1[None, :], axis=1))
    dlog = (
        weighted
        - factor * plan * dg2[None, :]
        - second * df2[:, None]
        - scaled * dg1[None, :]
        - first * df1[:, None]
    )
    dscore = INV_EPS * dlog
    grad_emb = lax.psum_scatter(
        jnp.dot(
            dscore, prototypes, precision=lax.Precision.HIGHEST, preferred_element_type=jnp.float32
        ),
        "comm",
        scatter_dimension=0,
        tiled=True,
    )
    grad_proto = lax.psum_scatter(
        lax.dot_general(
            dscore,
            embeddings,
            (((0,), (0,)), ((), ())),
            precision=lax.Precision.HIGHEST,
            preferred_element_type=jnp.float32,
        ),
        "node",
        scatter_dimension=0,
        tiled=True,
    )
    return (grad_emb, grad_proto)


def solution(mesh):
    in_specs = (P("node", None), P("comm", None), P("node", "comm"))
    out_specs = (P(("node", "comm"), None), P(("comm", "node"), None))
    return jax.shard_map(
        on_device, mesh=mesh, in_specs=in_specs, out_specs=out_specs, check_vma=False
    )
```

profile of v0, /device:TPU:6, one launch (start us, length us, event | category | flops | bytes accessed | tf_op | source)
XLA Modules:
  0.0 1245.5 jit_solution(11185800686010689899)
XLA Ops:
  8.0 0.0 copy-start
  8.0 0.0 all-reduce.3.cloned.1.call-start
  8.1 1.2 copy-done
  9.2 6.0 fusion.4
  15.2 15.1 %pmax.28 = f32[2048]{0:T(1024)S(1)} all-reduce(f32[2048]{0:T(1024)S(1)} %get-tuple-element.6), channel_id=1, replica_groups=mesh['comm'=8,'node'=64] {'comm'}, use_global_device_ids=true, to_apply=%region_1.0 | all-reduce | flops 2048 | bytes 16384 | tf_op jit(solution)/shard_map/pmax | solution.py:12
  30.3 2.8 exponential_reduce_fusion.3
  33.1 12.7 %psum.56 = f32[2048]{0:T(1024)S(1)} all-reduce(f32[2048]{0:T(1024)S(1)} %exponential_reduce_fusion.3), channel_id=1, replica_groups=mesh['comm'=8,'node'=64] {'comm'}, use_global_device_ids=true, to_apply=%region_3.0 | all-reduce | flops 2048 | bytes 16384 | tf_op jit(solution)/shard_map/psum | solution.py:13
  45.8 2.5 add_reduce_fusion.1
  48.3 141.7 %pmax.29 = f32[512]{0:T(512)S(1)} all-reduce(f32[512]{0:T(512)S(1)} %add_reduce_fusion.1), channel_id=1, replica_groups=mesh['comm'=8,'node'=64] {'node'}, use_global_device_ids=true, to_apply=%region_5.0 | all-reduce | flops 512 | bytes 4096 | tf_op jit(solution)/shard_map/pmax | solution.py:18
  190.0 3.0 exponential_reduce_fusion.2
  193.0 142.5 %psum.57 = f32[512]{0:T(512)S(1)} all-reduce(f32[512]{0:T(512)S(1)} %exponential_reduce_fusion.2), channel_id=1, replica_groups=mesh['comm'=8,'node'=64] {'node'}, use_global_device_ids=true, to_apply=%region_7.0 | all-reduce | flops 512 | bytes 4096 | tf_op jit(solution)/shard_map/psum | solution.py:19
  335.5 2.5 add_reduce_fusion
  338.0 12.7 %pmax.30 = f32[2048]{0:T(1024)S(1)} all-reduce(f32[2048]{0:T(1024)S(1)} %add_reduce_fusion), channel_id=1, replica_groups=mesh['comm'=8,'node'=64] {'comm'}, use_global_device_ids=true, to_apply=%region_9.0 | all-reduce | flops 2048 | bytes 16384 | tf_op jit(solution)/shard_map/pmax | solution.py:12
  350.7 3.0 exponential_reduce_fusion.1
  353.7 12.7 %psum.58 = f32[2048]{0:T(1024)S(1)} all-reduce(f32[2048]{0:T(1024)S(1)} %exponential_reduce_fusion.1), channel_id=1, replica_groups=mesh['comm'=8,'node'=64] {'comm'}, use_global_device_ids=true, to_apply=%region_11.0 | all-reduce | flops 2048 | bytes 16384 | tf_op jit(solution)/shard_map/psum | solution.py:13
  366.4 2.5 add_reduce_fusion.2
  368.9 138.0 %pmax.31 = f32[512]{0:T(512)S(1)} all-reduce(f32[512]{0:T(512)S(1)} %add_reduce_fusion.2), channel_id=1, replica_groups=mesh['comm'=8,'node'=64] {'node'}, use_global_device_ids=true, to_apply=%region_13.0 | all-reduce | flops 512 | bytes 4096 | tf_op jit(solution)/shard_map/pmax | solution.py:18
  506.9 3.0 exponential_reduce_fusion
  509.9 140.0 %psum.59 = f32[512]{0:T(512)S(1)} all-reduce(f32[512]{0:T(512)S(1)} %exponential_reduce_fusion), channel_id=1, replica_groups=mesh['comm'=8,'node'=64] {'node'}, use_global_device_ids=true, to_apply=%region_15.0 | all-reduce | flops 512 | bytes 4096 | tf_op jit(solution)/shard_map/psum | solution.py:19
  649.9 2.9 copy.6
  652.8 3.5 fusion.2
  656.3 138.0 %psum.60 = f32[512]{0:T(512)S(1)} all-reduce(f32[512]{0:T(512)S(1)} %get-tuple-element.2), channel_id=1, replica_groups=mesh['comm'=8,'node'=64] {'node'}, use_global_device_ids=true, to_apply=%region_17.0 | all-reduce | flops 512 | bytes 4096 | tf_op jit(solution)/shard_map/psum | solution.py:28
  794.3 3.1 multiply_reduce_fusion
  797.4 12.7 %psum.61 = f32[2048]{0:T(1024)S(1)} all-reduce(f32[2048]{0:T(1024)S(1)} %multiply_subtract_fusion), channel_id=1, replica_groups=mesh['comm'=8,'node'=64] {'comm'}, use_global_device_ids=true, to_apply=%region_20.0 | all-reduce | flops 2048 | bytes 16384 | tf_op jit(solution)/shard_map/psum | solution.py:24
  810.1 3.1 fusion.3
  813.2 140.0 %psum.62 = f32[512]{0:T(512)S(1)} all-reduce(f32[512]{0:T(512)S(1)} %fusion.3), channel_id=1, replica_groups=mesh['comm'=8,'node'=64] {'node'}, use_global_device_ids=true, to_apply=%region_22.0 | all-reduce | flops 512 | bytes 4096 | tf_op jit(solution)/shard_map/psum | solution.py:28
  953.2 3.1 fusion
  956.3 12.8 %psum.63 = f32[2048]{0:T(1024)S(1)} all-reduce(f32[2048]{0:T(1024)S(1)} %fusion), channel_id=1, replica_groups=mesh['comm'=8,'node'=64] {'comm'}, use_global_device_ids=true, to_apply=%region_24.0 | all-reduce | flops 2048 | bytes 16384 | tf_op jit(solution)/shard_map/psum | solution.py:24
  969.1 5.7 subtract_multiply_fusion
  974.8 0.0 copy-start.1
  974.8 1.9 copy-done.1
  976.8 0.0 copy-start.2
  976.8 4.2 fusion.6
  980.9 0.0 all-reduce.3.cloned.1.call-update
  980.9 0.0 reduce-scatter.2.cloned.1.call-start
  981.0 0.0 copy-done.2
  981.0 9.9 fusion.5
  990.9 0.0 reduce-scatter.2.cloned.1.call-update
  990.9 1.3 dynamic-slice
  992.8 244.0 %all-reduce.3.cloned.1.call-done = f32[512,128]{1,0:T(8,128)} async-done(((f32[512,128]{1,0:T(8,128)}), f32[512,128]{1,0:T(8,128)}) %all-reduce.3.cloned.1.call-update) | async-done | bytes 262160
  1236.8 1.3 constant_dynamic-slice_fusion
  1238.1 0.0 reduce-scatter.2.cloned.1.call-done
  (8 shorter events, 0.1 us)
Async XLA Ops:
  8.0 1.2 copy-start
  8.0 1228.8 %all-reduce.3.cloned.1.call-start = ((), (), s32[]{:S(2)}) async-start(), calls=%async_computation.2 | async-start | bytes 524288
  974.8 1.9 copy-start.1
  976.8 4.2 copy-start.2
  980.9 257.2 %reduce-scatter.2.cloned.1.call-start = ((), (), s32[]{:S(2)}) async-start(), calls=%async_computation.1 | async-start | bytes 1179648 | tf_op jit(solution)/shard_map/reduce_scatter | solution.py:68
Sparse Core Ops, SparseCore 0:
  981.1 255.7 all-reduce.2
Sparse Core Ops, SparseCore 1:
  991.0 34.9 reduce-scatter.1
where the time goes:
time: 1250 us
  blocking collectives  919 us (74%)
  waiting for transfers between devices  244 us (20%)
  other arithmetic  37.9 us (3%)
  matrix products  20 us (2%)
  between operations  16.3 us (1%)
    psum x2, blocking collectives, col_lse(): mass = lax.psum(jnp.sum(jnp.exp(shifted - peak[None, :]), axis=0), 'node')  282 us
    pmax x2, blocking collectives, col_lse(): peak = lax.pmax(jnp.max(shifted, axis=0), 'node')  280 us
    psum x2, blocking collectives, col_total(): return lax.psum(values, 'node')  278 us
    unnamed x3, waiting for transfers between devices  244 us
    pmax x2, blocking collectives, row_lse(): peak = lax.pmax(jnp.max(shifted, axis=1), 'comm')  27.8 us
    psum x2, blocking collectives, row_total(): return lax.psum(values, 'comm')  25.5 us
    psum x2, blocking collectives, row_lse(): mass = lax.psum(jnp.sum(jnp.exp(shifted - peak[:, None]), axis=1), 'comm')  25.3 us
  transfers between devices with their start and end apart: 2, of which 1 were waited for; matrix products, arithmetic and copies ran while one was open for 1% of the time, Pallas kernels for 0%

commit v1 on v0

v1 whole, which is shorter than its diff:
```python
import math

import jax
import jax.numpy as jnp
from jax import lax
from jax.sharding import PartitionSpec as P

INV_EPS = 20.0


def to_all(values, axis):
    count = lax.axis_size(axis)
    copies = jnp.broadcast_to(values[None], (count,) + values.shape)
    return lax.all_to_all(copies, axis, 0, 0, tiled=True)


def merge(parts):
    peak = jnp.max(parts, axis=0)
    share = jnp.exp(parts - peak[None])
    mass = jnp.sum(share, axis=0)
    return peak + jnp.log(mass), share / mass[None]


def row_lse(shifted):
    peak = jnp.max(shifted, axis=1)
    mass = jnp.sum(jnp.exp(shifted - peak[:, None]), axis=1)
    return merge(to_all(peak + jnp.log(mass), "comm"))[0]


def scatter_sum(terms, axis):
    count = lax.axis_size(axis)
    blocks = terms.reshape(count, terms.shape[0] // count, terms.shape[1])
    return jnp.sum(lax.all_to_all(blocks, axis, 0, 0, tiled=True), axis=0)


def on_device(embeddings, prototypes, plan_grad):
    rows = embeddings.shape[0]
    local = prototypes.shape[0]
    comm_count = lax.axis_size("comm")
    node_count = lax.axis_size("node")
    per_proto = (rows * node_count) / (local * comm_count)
    log_mass = math.log(per_proto)
    factor = 1.0 / per_proto
    grads = plan_grad.astype(jnp.float32)
    logits = (
        jnp.dot(
            embeddings,
            prototypes.T,
            precision=lax.Precision.HIGHEST,
            preferred_element_type=jnp.float32,
        )
        * INV_EPS
    )
    f1 = -row_lse(logits)
    moved = logits + f1[:, None]
    peak = jnp.max(moved, axis=0)
    mass = jnp.sum(jnp.exp(moved - peak[None, :]), axis=0)
    g1 = log_mass - merge(to_all(peak + jnp.log(mass), "node"))[0]
    f2 = -row_lse(logits + g1[None, :])
    moved = logits + f2[:, None]
    peak = jnp.max(moved, axis=0)
    terms = jnp.exp(moved - peak[None, :])
    mass = jnp.sum(terms, axis=0)
    mean = jnp.sum(grads * terms, axis=0) / mass
    both = to_all(jnp.stack([peak + jnp.log(mass), mean]), "node")
    total, share = merge(both[:, 0])
    g2 = log_mass - total
    dg2 = per_proto * jnp.sum(share * both[:, 1], axis=0)
    plan = jnp.exp(logits + f2[:, None] + g2[None, :])
    df2 = jnp.sum(plan * (grads - factor * dg2[None, :]), axis=1)
    df2 = jnp.sum(to_all(df2, "comm"), axis=0)
    second = jnp.exp(logits + f2[:, None] + g1[None, :])
    dg1 = -jnp.sum(to_all(jnp.sum(second * df2[:, None], axis=0), "node"), axis=0)
    scaled = jnp.exp(logits + f1[:, None] + (g1 - log_mass)[None, :])
    df1 = -jnp.sum(to_all(jnp.sum(scaled * dg1[None, :], axis=1), "comm"), axis=0)
    first = jnp.exp(logits + f1[:, None])
    dscore = INV_EPS * (
        plan * (grads - factor * dg2[None, :])
        - second * df2[:, None]
        - scaled * dg1[None, :]
        - first * df1[:, None]
    )
    grad_proto = lax.dot_general(
        dscore,
        embeddings,
        (((0,), (0,)), ((), ())),
        precision=lax.Precision.HIGHEST,
        preferred_element_type=jnp.float32,
    )
    grad_emb = jnp.dot(
        dscore, prototypes, precision=lax.Precision.HIGHEST, preferred_element_type=jnp.float32
    )
    return scatter_sum(grad_emb, "comm"), scatter_sum(grad_proto, "node")


def solution(mesh):
    in_specs = (P("node", None), P("comm", None), P("node", "comm"))
    out_specs = (P(("node", "comm"), None), P(("comm", "node"), None))
    return jax.shard_map(
        on_device, mesh=mesh, in_specs=in_specs, out_specs=out_specs, check_vma=False
    )
```

time: 1250 us -> 210 us (0.17)
  blocking collectives: 919 us -> 117 us
  waiting for transfers between devices: 244 us -> 27 us
  between operations: 16.3 us -> 0.9 us
    psum x8 -> x0, blocking collectives: 611 us -> none  [the longest x2 282 us: col_lse(): mass = lax.psum(jnp.sum(jnp.exp(shifted - peak[None, :]), axis=0), 'node')]
    pmax x4 -> x0, blocking collectives: 307 us -> none  [the longest x2 280 us: col_lse(): peak = lax.pmax(jnp.max(shifted, axis=0), 'node')]
    unnamed x3 -> x0, waiting for transfers between devices: 244 us -> none
    all_to_all x0 -> x7, blocking collectives: none -> 117 us  [to_all(): return lax.all_to_all(copies, axis, 0, 0, tiled=True)]
    all_to_all x0 -> x2, waiting for transfers between devices: none -> 27 us  [scatter_sum(): return jnp.sum(lax.all_to_all(blocks, axis, 0, 0, tiled=True), axis=0)]
  transfers between devices with their start and end apart: 2 -> 2, of which waited for: 1 -> 2; matrix products, arithmetic and copies ran while one was open for 1% -> 5% of each run, Pallas kernels for 0% -> 0%
where the time goes in v1:
time: 210 us; the launch traced here: 209 us
  blocking collectives  117 us (56%)
  other arithmetic  28.4 us (14%)
  waiting for transfers between devices  27 us (13%)
  matrix products  18.7 us (9%)
  starting transfers between devices  10.2 us (5%)
  local copies, waits for them, and re-layouts  7.48 us (4%)
    all_to_all x7, blocking collectives, to_all(): return lax.all_to_all(copies, axis, 0, 0, tiled=True)  117 us
    all_to_all x2, waiting for transfers between devices, scatter_sum(): return jnp.sum(lax.all_to_all(blocks, axis, 0, 0, tiled=True), axis=0)  27 us
    all_to_all x2, starting transfers between devices, scatter_sum(): return jnp.sum(lax.all_to_all(blocks, axis, 0, 0, tiled=True), axis=0)  10.2 us
    dot_general x1, matrix products, on_device(): lax.dot_general(dscore, embeddings, (((0,), (0,)), ((), ())), precision=l...  9.55 us
    unnamed x16, local copies, waits for them, and re-layouts  7.12 us
    mul x1, other arithmetic, on_device(): INV_EPS * (plan * (grads - factor * dg2[None, :]) - second * df2[:, None]...  5.48 us
    reduce_max x2, other arithmetic, on_device(): peak = jnp.max(moved, axis=0)  5.38 us
    dot_general x1, matrix products, on_device(): jnp.dot(embeddings, prototypes.T, precision=lax.Precision.HIGHEST, prefer...  4.62 us
  transfers between devices with their start and end apart: 2, of which 2 were waited for; matrix products, arithmetic and copies ran while one was open for 5% of the time, Pallas kernels for 0%

profile of v1, /device:TPU:6, one launch (start us, length us, event | category | flops | bytes accessed | tf_op | source)
XLA Modules:
  0.0 209.4 jit_solution(9524756182256212409)
XLA Ops:
  0.6 0.0 copy-start
  0.6 1.2 copy-done
  1.9 4.6 %fusion.16 = (f32[2048]{0:T(1024)S(1)}, f32[2048,512]{1,0:T(8,128)S(1)}) fusion(f32[2048,128]{1,0:T(8,128)S(1)} %copy-done, f32[512,128]{1,0:T(8,128)} %param.4), kind=kOutput, calls=%fused_computation.47 | convolution fusion | flops 1612707840 | bytes 5513216 | tf_op jit(solution)/shard_map/dot_general | solution.py:46
  6.5 1.9 copy-done.1
  8.4 1.7 exponential_reduce_fusion.2
  10.2 9.9 %all_to_all.60 = f32[8,1,2048]{2,1,0:T(1,128)S(1)} all-to-all(f32[8,1,2048]{2,1,0:T(1,128)S(1)} %broadcast_in_dim.14), channel_id=1, replica_groups=mesh['comm'=8,'node'=64] {'comm'}, dimensions={0} | all-to-all | bytes 131072 | tf_op jit(solution)/shard_map/all_to_all | solution.py:14
  20.1 0.1 reduce_max.73
  20.1 0.0 copy-start.2
  20.2 2.7 %add_reduce_fusion.1 = f32[512]{0:T(512)S(1)} fusion(f32[2048,512]{1,0:T(8,128)} %copy-done.1, f32[2048]{0:T(1024)S(1)} %add_negate_fusion.1), kind=kLoop, calls=%fused_computation.15 | loop fusion | flops 2096640 | bytes 4204544 | tf_op jit(solution)/shard_map/reduce_max | solution.py:56
  22.9 0.7 copy-done.2
  23.6 0.8 exponential_reduce_fusion.1
  24.3 0.1 broadcast_in_dim.15
  24.4 34.0 %all_to_all.61 = f32[64,1,512]{2,1,0:T(1,128)S(1)} all-to-all(f32[64,1,512]{2,1,0:T(1,128)S(1)} %broadcast_in_dim.15), channel_id=1, replica_groups=mesh['comm'=8,'node'=64] {'node'}, dimensions={0} | all-to-all | bytes 262144 | tf_op jit(solution)/shard_map/all_to_all | solution.py:14
  58.5 0.1 reduce_max.75
  58.6 2.7 %add_reduce_fusion = f32[2048]{0:T(1024)S(1)} fusion(f32[2048,512]{1,0:T(8,128)} %copy-done.1, f32[512]{0:T(512)S(1)} %get-tuple-element.8), kind=kLoop, calls=%fused_computation.12 | loop fusion | flops 2095104 | bytes 4204544 | tf_op jit(solution)/shard_map/reduce_max | solution.py:25
  61.3 0.7 copy-done.3
  62.0 1.3 exponential_reduce_fusion
  63.4 8.0 %all_to_all.62 = f32[8,1,2048]{2,1,0:T(1,128)S(1)} all-to-all(f32[8,1,2048]{2,1,0:T(1,128)S(1)} %broadcast_in_dim.16), channel_id=1, replica_groups=mesh['comm'=8,'node'=64] {'comm'}, dimensions={0} | all-to-all | bytes 131072 | tf_op jit(solution)/shard_map/all_to_all | solution.py:14
  71.4 0.1 reduce_max.77
  71.4 0.0 copy-start.4
  71.5 2.7 %add_reduce_fusion.2 = f32[512]{0:T(512)S(1)} fusion(f32[2048,512]{1,0:T(8,128)} %copy-done.1, f32[2048]{0:T(1024)S(1)} %add_negate_fusion), kind=kLoop, calls=%fused_computation.17 | loop fusion | flops 2096640 | bytes 4204544 | tf_op jit(solution)/shard_map/reduce_max | solution.py:61
  74.2 0.7 copy-done.4
  74.9 1.3 fusion.3
  76.2 0.1 broadcast_in_dim.17
  76.3 27.4 %all_to_all.63 = f32[64,2,512]{2,1,0:T(2,128)S(1)} all-to-all(f32[64,2,512]{2,1,0:T(2,128)S(1)} %broadcast_in_dim.17), channel_id=1, replica_groups=mesh['comm'=8,'node'=64] {'node'}, dimensions={0} | all-to-all | bytes 524288 | tf_op jit(solution)/shard_map/all_to_all | solution.py:14
  103.7 0.3 slice_reduce_fusion
  104.0 0.1 fusion.8
  104.0 1.5 fusion.5
  105.6 8.0 %all_to_all.64 = f32[8,1,2048]{2,1,0:T(1,128)S(1)} all-to-all(f32[8,1,2048]{2,1,0:T(1,128)S(1)} %broadcast_in_dim.18), channel_id=1, replica_groups=mesh['comm'=8,'node'=64] {'comm'}, dimensions={0} | all-to-all | bytes 131072 | tf_op jit(solution)/shard_map/all_to_all | solution.py:14
  113.6 0.1 reduce_sum.173
  113.6 2.7 %fusion.4 = f32[512]{0:T(512)S(1)} fusion(f32[2048,512]{1,0:T(8,128)} %copy-done.1, f32[2048]{0:T(1024)S(1)} %reduce_sum.173, f32[2048]{0:T(1024)S(1)} %add_negate_fusion, f32[512]{0:T(512)S(1)} %get-tuple-element.8), kind=kLoop, calls=%fused_computation.14 | loop fusion | flops 4193792 | bytes 4214784 | tf_op jit(solution)/shard_map/reduce_sum | solution.py:73
  116.3 0.1 broadcast_in_dim.19
  116.4 21.4 %all_to_all.65 = f32[64,1,512]{2,1,0:T(1,128)S(1)} all-to-all(f32[64,1,512]{2,1,0:T(1,128)S(1)} %broadcast_in_dim.19), channel_id=1, replica_groups=mesh['comm'=8,'node'=64] {'node'}, dimensions={0} | all-to-all | bytes 262144 | tf_op jit(solution)/shard_map/all_to_all | solution.py:14
  137.8 0.1 reduce_sum.175
  138.0 3.2 %fusion.2 = f32[2048]{0:T(1024)S(1)} fusion(f32[2048,512]{1,0:T(8,128)} %copy-done.1, f32[512]{0:T(512)S(1)} %neg.30, f32[512]{0:T(512)S(1)} %get-tuple-element.7, f32[2048]{0:T(1024)S(1)} %add_negate_fusion.1), kind=kLoop, calls=%fused_computation.6 | loop fusion | flops 4192256 | bytes 4214784 | tf_op jit(solution)/shard_map/reduce_sum | solution.py:75
  141.2 8.0 %all_to_all.66 = f32[8,1,2048]{2,1,0:T(1,128)S(1)} all-to-all(f32[8,1,2048]{2,1,0:T(1,128)S(1)} %broadcast_in_dim.20), channel_id=1, replica_groups=mesh['comm'=8,'node'=64] {'comm'}, dimensions={0} | all-to-all | bytes 131072 | tf_op jit(solution)/shard_map/all_to_all | solution.py:14
  149.2 0.1 reduce_sum.177
  149.3 0.0 copy-start.7
  149.3 5.5 %subtract_multiply_fusion = f32[2048,512]{1,0:T(8,128)S(1)} fusion(f32[2048,512]{1,0:T(8,128)} %copy-done.1, bf16[2048,512]{1,0:T(8,128)(2,1)S(1)} %copy-done.6, f32[2048]{0:T(1024)S(1)} %neg.31, f32[512]{0:T(512)S(1)} %neg.30, f32[512]{0:T(512)S(1)} %get-tuple-element.7, f32[2048]{0:T(1024)S(1)} %reduce_sum.173, f32[512]{0:T(512)S(1)} %fusion.8, ...), kind=kLoop, calls=%fused_computation.4 | loop fusion | flops 15728640 | bytes 10528768 | tf_op jit(solution)/shard_map/mul | solution.py:77
  154.8 1.9 copy-done.5
  156.7 4.5 %fusion.17 = f32[2048,128]{1,0:T(8,128)} fusion(f32[2048,512]{1,0:T(8,128)S(1)} %subtract_multiply_fusion, f32[512,128]{1,0:T(8,128)S(1)} %copy-done.7), kind=kOutput, calls=%fused_computation.48 | convolution fusion | flops 1610612736 | bytes 5505024 | tf_op jit(solution)/shard_map/dot_general | solution.py:90
  161.2 3.8 %all-to-all-start.7 = ((f32[8,256,128]{2,1,0:T(8,128)}), f32[8,256,128]{2,1,0:T(8,128)S(1)}, u32[]{:S(2)}, u32[]{:S(2)}) async-start(f32[8,256,128]{2,1,0:T(8,128)} %bitcast.3), calls=%async_computation.7 | async-start | bytes 2097152 | tf_op jit(solution)/shard_map/all_to_all | solution.py:33
  165.0 9.6 %convolution_bitcast_fusion = f32[64,8,128]{2,1,0:T(8,128)} fusion(f32[2048,512]{1,0:T(8,128)} %copy-done.5, f32[2048,128]{1,0:T(8,128)S(1)} %copy-done), kind=kOutput, calls=%fused_computation.19 | convolution fusion | flops 1610612736 | bytes 5505024 | tf_op jit(solution)/shard_map/dot_general | solution.py:83
  174.5 6.1 %all-to-all-done.7 = f32[8,256,128]{2,1,0:T(8,128)S(1)} async-done(((f32[8,256,128]{2,1,0:T(8,128)}), f32[8,256,128]{2,1,0:T(8,128)S(1)}, u32[]{:S(2)}, u32[]{:S(2)}) %all-to-all-start.7) | async-done | bytes 1048608 | tf_op jit(solution)/shard_map/all_to_all | solution.py:33
  180.6 6.4 %all-to-all-start.8 = ((f32[64,8,128]{2,1,0:T(8,128)}), f32[64,8,128]{2,1,0:T(8,128)S(1)}, u32[]{:S(2)}, u32[]{:S(2)}) async-start(f32[64,8,128]{2,1,0:T(8,128)} %convolution_bitcast_fusion), calls=%async_computation.8 | async-start | bytes 524288 | tf_op jit(solution)/shard_map/all_to_all | solution.py:33
  187.1 0.7 reduce_sum.178
  187.8 20.9 %all-to-all-done.8 = f32[64,8,128]{2,1,0:T(8,128)S(1)} async-done(((f32[64,8,128]{2,1,0:T(8,128)}), f32[64,8,128]{2,1,0:T(8,128)S(1)}, u32[]{:S(2)}, u32[]{:S(2)}) %all-to-all-start.8) | async-done | bytes 262176 | tf_op jit(solution)/shard_map/all_to_all | solution.py:33
  208.7 0.7 reduce_sum.179
  (25 shorter events, 0.4 us)
Async XLA Ops:
  0.6 1.2 copy-start
  6.5 1.9 copy-start.1
  20.1 3.5 %copy-start.2 = (f32[2048,512]{1,0:T(8,128)S(1)}, f32[2048,512]{1,0:T(8,128)}, u32[]{:S(2)}) copy-start(f32[2048,512]{1,0:T(8,128)} %copy-done.1) | copy-start | bytes 12582916
  58.6 3.4 %copy-start.3 = (f32[2048,512]{1,0:T(8,128)S(1)}, f32[2048,512]{1,0:T(8,128)}, u32[]{:S(2)}) copy-start(f32[2048,512]{1,0:T(8,128)} %copy-done.1) | copy-start | bytes 12582916
  62.0 12.2 %copy-start.6 = (bf16[2048,512]{1,0:T(8,128)(2,1)S(1)}, bf16[2048,512]{1,0:T(8,128)(2,1)}, u32[]{:S(2)}) copy-start(bf16[2048,512]{1,0:T(8,128)(2,1)} %param.5) | copy-start | bytes 6291460
  71.4 3.5 %copy-start.4 = (f32[2048,512]{1,0:T(8,128)S(1)}, f32[2048,512]{1,0:T(8,128)}, u32[]{:S(2)}) copy-start(f32[2048,512]{1,0:T(8,128)} %copy-done.1) | copy-start | bytes 12582916
  149.3 7.4 %copy-start.7 = (f32[512,128]{1,0:T(8,128)S(1)}, f32[512,128]{1,0:T(8,128)}, u32[]{:S(2)}) copy-start(f32[512,128]{1,0:T(8,128)} %param.4) | copy-start | bytes 786436
  154.8 1.9 copy-start.5
  161.2 19.4 %all-to-all-start.7 = ((f32[8,256,128]{2,1,0:T(8,128)}), f32[8,256,128]{2,1,0:T(8,128)S(1)}, u32[]{:S(2)}, u32[]{:S(2)}) async-start(f32[8,256,128]{2,1,0:T(8,128)} %bitcast.3), calls=%async_computation.7 | async-start | bytes 2097152 | tf_op jit(solution)/shard_map/all_to_all | solution.py:33
  180.6 28.1 %all-to-all-start.8 = ((f32[64,8,128]{2,1,0:T(8,128)}), f32[64,8,128]{2,1,0:T(8,128)S(1)}, u32[]{:S(2)}, u32[]{:S(2)}) async-start(f32[64,8,128]{2,1,0:T(8,128)} %convolution_bitcast_fusion), calls=%async_computation.8 | async-start | bytes 524288 | tf_op jit(solution)/shard_map/all_to_all | solution.py:33

commit v2 on v1

v2 whole, which is shorter than its diff:
```python
import math

import jax
import jax.numpy as jnp
from jax import lax
from jax.experimental import pallas as pl
from jax.experimental.pallas import tpu as pltpu
from jax.sharding import PartitionSpec as P

INV_EPS = 20.0
LOG2E = 1.0 / math.log(2.0)
LANES = 128
WIDE = 256
SPAN = 8
F32 = jnp.float32
BF16 = jnp.bfloat16
NT = (((1,), (1,)), ((), ()))
EVERY = slice(None)


def to_all(values, axis):
    count = lax.axis_size(axis)
    copies = jnp.broadcast_to(values[None], (count,) + values.shape)
    return lax.all_to_all(copies, axis, 0, 0, tiled=True)


def scatter_sum(terms, axis):
    count = lax.axis_size(axis)
    blocks = terms.reshape(count, terms.shape[0] // count, terms.shape[1])
    return jnp.sum(lax.all_to_all(blocks, axis, 0, 0, tiled=True), axis=0)


def split(x, pieces):
    out = []
    for _ in range(pieces):
        piece = x.astype(BF16)
        out.append(piece)
        x = x - piece.astype(F32)
    return out


def down(row):
    return jnp.transpose(jnp.broadcast_to(row, (LANES, row.shape[1])))


def tile_rows(at, tall):
    return pl.ds(pl.multiple_of(at * tall, tall), tall)


def lanes_of(ref, rows, tile):
    return ref[rows, tile * LANES : (tile + 1) * LANES]


def add_parts(parts):
    values = [parts[k] for k in range(parts.shape[0])]
    while len(values) > 1:
        values = [a + b for a, b in zip(values[::2], values[1::2])]
    return values[0]


def merge_parts(parts):
    count = parts.shape[0]
    peak = parts[0, 0:1, :]
    for k in range(1, count):
        peak = jnp.maximum(peak, parts[k, 0:1, :])
    mass = jnp.zeros(peak.shape, F32)
    mean = jnp.zeros(peak.shape, F32)
    for k in range(count):
        share = jnp.exp2(parts[k, 0:1, :] - peak)
        mass = mass + share
        if parts.shape[1] == 2:
            mean = mean + share * parts[k, 1:2, :]
    total = peak + jnp.log2(mass)
    return total if parts.shape[1] == 1 else (total, mean / mass)


def scores_kernel(emb, proto, grads, logits, turned, row_out, e_in, p_in, g_in, sems):
    chunks = 4
    size = emb.shape[0] // chunks
    get_p = pltpu.make_async_copy(proto, p_in, sems.at[0])
    get_p.start()
    get_e = []
    for k in range(chunks):
        rows = pl.ds(k * size, size)
        get_e.append(pltpu.make_async_copy(emb.at[rows], e_in.at[rows], sems.at[1 + k]))
        get_e[k].start()
    get_g = pltpu.make_async_copy(grads, g_in, sems.at[1 + chunks])
    get_g.start()
    get_p.wait()
    hi, mid, low = split(p_in[...] * (INV_EPS * LOG2E), 3)
    left = jnp.concatenate([hi, hi, hi, mid, mid, low], axis=1)
    for at in range(0, emb.shape[0], WIDE):
        if at % size == 0:
            get_e[at // size].wait()
        hi, mid, low = split(e_in[at : at + WIDE, :], 3)
        right = jnp.concatenate([hi, mid, low, hi, mid, hi], axis=1)
        tile = lax.dot_general(left, right, NT, preferred_element_type=F32)
        logits[:, at : at + WIDE] = tile
        peak = jnp.max(tile, axis=0, keepdims=True)
        mass = jnp.sum(jnp.exp2(tile - peak), axis=0, keepdims=True)
        row_out[:, at : at + WIDE] = peak + jnp.log2(mass)
    eye = (
        lax.broadcasted_iota(jnp.int32, (WIDE, WIDE), 0)
        == lax.broadcasted_iota(jnp.int32, (WIDE, WIDE), 1)
    ).astype(F32).astype(BF16)
    get_g.wait()
    for at in range(0, grads.shape[1], WIDE):
        turned[at : at + WIDE, :] = lax.dot_general(
            eye, g_in[:, at : at + WIDE], NT, preferred_element_type=F32
        ).astype(BF16)


def col_kernel(logits, parts, f1, lse_out, shifts, peaks, masses):
    tiles = logits.shape[1] // LANES
    f1[...] = -merge_parts(parts)
    shifts[...] = jnp.broadcast_to(f1[...], shifts.shape)

    def step(at, _):
        rows = tile_rows(at, 8)
        moved = [lanes_of(logits, rows, k) + lanes_of(shifts, EVERY, k) for k in range(tiles)]
        peak = moved[0]
        for part in moved[1:]:
            peak = jnp.maximum(peak, part)
        mass = jnp.exp2(moved[0] - peak)
        for part in moved[1:]:
            mass = mass + jnp.exp2(part - peak)
        peaks[rows, :] = peak
        masses[rows, :] = mass
        return 0

    lax.fori_loop(0, logits.shape[0] // 8, step, 0, unroll=4)
    peak_t = jnp.transpose(peaks[...])
    peak = jnp.max(peak_t, axis=0, keepdims=True)
    mass = jnp.sum(jnp.transpose(masses[...]) * jnp.exp2(peak_t - peak), axis=0, keepdims=True)
    lse_out[...] = peak + jnp.log2(mass)


def col_mean_kernel(logits, parts, grads, f2, out, shifts, peaks, masses, means):
    tiles = logits.shape[1] // LANES
    f2[...] = -merge_parts(parts)
    shifts[...] = jnp.broadcast_to(f2[...], shifts.shape)

    def step(at, _):
        rows = tile_rows(at, 16)
        peak = lanes_of(logits, rows, 0) + lanes_of(shifts, EVERY, 0)
        for k in range(1, tiles):
            peak = jnp.maximum(peak, lanes_of(logits, rows, k) + lanes_of(shifts, EVERY, k))
        mass = jnp.zeros((16, LANES), F32)
        mean = jnp.zeros((16, LANES), F32)
        for k in range(tiles):
            term = jnp.exp2(lanes_of(logits, rows, k) + lanes_of(shifts, EVERY, k) - peak)
            mass = mass + term
            mean = mean + term * lanes_of(grads, rows, k).astype(F32)
        peaks[rows, :] = peak
        masses[rows, :] = mass
        means[rows, :] = mean
        return 0

    lax.fori_loop(0, logits.shape[0] // 16, step, 0, unroll=2)
    peak_t = jnp.transpose(peaks[...])
    peak = jnp.max(peak_t, axis=0, keepdims=True)
    share = jnp.exp2(peak_t - peak)
    mass = jnp.sum(jnp.transpose(masses[...]) * share, axis=0, keepdims=True)
    mean = jnp.sum(jnp.transpose(means[...]) * share, axis=0, keepdims=True)
    out[0:1, :] = peak + jnp.log2(mass)
    out[1:2, :] = mean / mass


def span_lanes(span, tile):
    start = pl.multiple_of(span * (SPAN * LANES), SPAN * LANES)
    return pl.ds(start + tile * LANES, LANES)


def row_kernel(log_mass, logits, parts, g1, lse_out, shifts):
    g1[...] = log_mass - merge_parts(parts)
    shifts[...] = down(g1[...])
    count = logits.shape[0] // 8

    def over(span, _):
        lanes = [span_lanes(span, k) for k in range(SPAN)]

        def highest(at, peak):
            rows = tile_rows(at, 8)
            move = shifts[rows, :]
            return [jnp.maximum(peak[k], logits[rows, lanes[k]] + move) for k in range(SPAN)]

        peak = lax.fori_loop(
            0, count, highest, [jnp.full((8, LANES), -jnp.inf, F32)] * SPAN, unroll=16
        )
        peak = [jnp.max(part, axis=0, keepdims=True) for part in peak]

        def add(at, mass):
            rows = tile_rows(at, 8)
            move = shifts[rows, :]
            return [
                mass[k] + jnp.exp2(logits[rows, lanes[k]] + move - peak[k]) for k in range(SPAN)
            ]

        mass = lax.fori_loop(0, count, add, [jnp.zeros((8, LANES), F32)] * SPAN, unroll=16)
        for k in range(SPAN):
            total = jnp.sum(mass[k], axis=0, keepdims=True)
            lse_out[:, lanes[k]] = peak[k] + jnp.log2(total)
        return 0

    lax.fori_loop(0, logits.shape[1] // (SPAN * LANES), over, 0)


def df2_kernel(log_mass, factor, logits, f2, parts, grads, score, out, cols, weights):
    total, mean = merge_parts(parts)
    cols[...] = down(log_mass - total)
    weights[...] = down(mean)
    tall = 16

    def over(span, _):
        lanes = [span_lanes(span, k) for k in range(SPAN)]
        moves = [f2[:, s] for s in lanes]

        def add(at, total):
            rows = tile_rows(at, tall)
            move = cols[rows, :]
            weigh = weights[rows, :]
            new = []
            for k in range(SPAN):
                term = jnp.exp2(logits[rows, lanes[k]] + move + moves[k])
                term = term * (grads[rows, lanes[k]].astype(F32) - weigh)
                score[rows, lanes[k]] = term
                new.append(total[k] + term[:8] + term[8:])
            return new

        total = lax.fori_loop(
            0, logits.shape[0] // tall, add, [jnp.zeros((8, LANES), F32)] * SPAN, unroll=4
        )
        for k in range(SPAN):
            out[:, lanes[k]] = jnp.sum(total[k], axis=0, keepdims=True)
        return 0

    lax.fori_loop(0, logits.shape[1] // (SPAN * LANES), over, 0)


def dg1_kernel(logits, f2, g1, parts, score, rest, out, rows_of, weights, cols, sums):
    tiles = logits.shape[1] // LANES
    rows_of[...] = jnp.broadcast_to(f2[...], rows_of.shape)
    weights[...] = jnp.broadcast_to(add_parts(parts), weights.shape)
    cols[...] = down(g1[...])

    def step(at, _):
        rows = tile_rows(at, 8)
        move = cols[rows, :]
        total = jnp.zeros((8, LANES), F32)
        for k in range(tiles):
            term = jnp.exp2(lanes_of(logits, rows, k) + lanes_of(rows_of, EVERY, k) + move)
            term = term * lanes_of(weights, EVERY, k)
            rest[rows, k * LANES : (k + 1) * LANES] = lanes_of(score, rows, k) - term
            total = total + term
        sums[rows, :] = total
        return 0

    lax.fori_loop(0, logits.shape[0] // 8, step, 0, unroll=4)
    out[...] = -jnp.sum(jnp.transpose(sums[...]), axis=0, keepdims=True)


def df1_kernel(log_mass, logits, f1, g1, parts, score, rest, out, cols, weights):
    cols[...] = down(g1[...] - log_mass)
    weights[...] = down(add_parts(parts))
    tall = 8

    def over(span, _):
        lanes = [span_lanes(span, k) for k in range(SPAN)]
        moves = [f1[:, s] for s in lanes]

        def add(at, total):
            rows = tile_rows(at, tall)
            move = cols[rows, :]
            weigh = weights[rows, :]
            new = []
            for k in range(SPAN):
                term = jnp.exp2(logits[rows, lanes[k]] + move + moves[k]) * weigh
                rest[rows, lanes[k]] = score[rows, lanes[k]] - term
                new.append(total[k] + term)
            return new

        total = lax.fori_loop(
            0, logits.shape[0] // tall, add, [jnp.zeros((tall, LANES), F32)] * SPAN, unroll=8
        )
        for k in range(SPAN):
            out[:, lanes[k]] = -jnp.sum(total[k], axis=0, keepdims=True)
        return 0

    lax.fori_loop(0, logits.shape[1] // (SPAN * LANES), over, 0)


def grads_kernel(logits, f1, parts, score, proto, emb, emb_out, proto_out, df1, work):
    width = proto.shape[1]
    df1[...] = add_parts(parts)
    p_hi, p_low = split(jnp.transpose(proto[...]) * INV_EPS, 2)
    p_both = jnp.concatenate([p_hi, p_low], axis=0)
    proto_out[...] = jnp.zeros(proto_out.shape, F32)

    def tile(at, _):
        start = pl.multiple_of(at * WIDE, WIDE)
        parts = range(WIDE // LANES)
        lanes = [pl.ds(start + k * LANES, LANES) for k in parts]
        moves = [f1[:, s] for s in lanes]
        weights = [df1[:, s] for s in lanes]

        def fill(group, _):
            rows = tile_rows(group, 8)
            for k in parts:
                first = jnp.exp2(logits[rows, lanes[k]] + moves[k])
                work[rows, k * LANES : (k + 1) * LANES] = (
                    score[rows, lanes[k]] - first * weights[k]
                )
            return 0

        lax.fori_loop(0, logits.shape[0] // 8, fill, 0, unroll=16)
        s_hi, s_low = split(work[...], 2)
        both = jnp.dot(p_both, s_hi, preferred_element_type=F32)
        emb_out[:, pl.ds(start, WIDE)] = (
            both[:width] + both[width:] + jnp.dot(p_hi, s_low, preferred_element_type=F32)
        )
        e_hi, e_low = split(emb[pl.ds(start, WIDE), :] * INV_EPS, 2)
        both = jnp.dot(s_hi, jnp.concatenate([e_hi, e_low], axis=1), preferred_element_type=F32)
        proto_out[...] += (
            both[:, :width] + both[:, width:] + jnp.dot(s_low, e_hi, preferred_element_type=F32)
        )
        return 0

    lax.fori_loop(0, logits.shape[1] // WIDE, tile, 0)


def call(kernel, name, outs, scratch, args, places=None):
    vmem = pl.BlockSpec(memory_space=pltpu.VMEM)
    return pl.pallas_call(
        kernel,
        name=name,
        out_shape=[jax.ShapeDtypeStruct(shape, dtype) for shape, dtype in outs],
        in_specs=places or [vmem] * len(args),
        out_specs=[vmem] * len(outs),
        scratch_shapes=[
            s if not isinstance(s, tuple) else pltpu.VMEM(s, F32) for s in scratch
        ],
        compiler_params=pltpu.CompilerParams(vmem_limit_bytes=24 * 2**20),
    )(*args)


def on_device(embeddings, prototypes, plan_grad):
    rows, width = embeddings.shape
    local = prototypes.shape[0]
    per_proto = (rows * lax.axis_size("node")) / (local * lax.axis_size("comm"))
    log_mass = math.log2(per_proto)
    factor = 1.0 / per_proto
    full = ((local, rows), F32)
    row = ((1, rows), F32)
    col = ((1, local), F32)
    tall = (local, LANES)
    hbm = pl.BlockSpec(memory_space=pltpu.HBM)

    logits, grads, here = call(
        scores_kernel, "scores", [full, ((local, rows), BF16), row],
        [(rows, width), (local, width), pltpu.VMEM((rows, local), BF16),
         pltpu.SemaphoreType.DMA((6,))],
        [embeddings, prototypes, plan_grad], [hbm] * 3,
    )
    f1, here = call(
        col_kernel, "col_lse", [row, col], [(8, rows), tall, tall],
        [logits, to_all(here, "comm")],
    )
    g1, here = call(
        lambda *refs: row_kernel(log_mass, *refs), "row_lse", [col, row], [tall],
        [logits, to_all(here, "node")],
    )
    f2, here = call(
        col_mean_kernel, "col_lse_mean", [row, ((2, local), F32)],
        [(16, rows), tall, tall, tall], [logits, to_all(here, "comm"), grads],
    )
    score, here = call(
        lambda *refs: df2_kernel(log_mass, factor, *refs), "df2", [full, row], [tall, tall],
        [logits, f2, to_all(here, "node"), grads],
    )
    score, here = call(
        dg1_kernel, "dg1", [full, col], [(8, rows), (8, rows), tall, tall],
        [logits, f2, g1, to_all(here, "comm"), score],
    )
    score, here = call(
        lambda *refs: df1_kernel(log_mass, *refs), "df1", [full, row], [tall, tall],
        [logits, f1, g1, to_all(here, "node"), score],
    )
    emb_part, proto_part = call(
        grads_kernel, "grads", [((width, rows), F32), ((local, width), F32)],
        [(1, rows), (local, WIDE)],
        [logits, f1, to_all(here, "comm"), score, prototypes, embeddings],
    )
    grad_emb = lax.psum_scatter(emb_part.T, "comm", scatter_dimension=0, tiled=True)
    grad_proto = scatter_sum(proto_part, "node")
    return grad_emb, grad_proto


def solution(mesh):
    in_specs = (P("node", None), P("comm", None), P("node", "comm"))
    out_specs = (P(("node", "comm"), None), P(("comm", "node"), None))
    return jax.shard_map(
        on_device, mesh=mesh, in_specs=in_specs, out_specs=out_specs, check_vma=False
    )
```

time: 210 us -> 190 us (0.905)
  other arithmetic: 28.4 us -> 0.66 us
  blocking collectives: 117 us -> 144 us
  waiting for transfers between devices: 27 us -> 2.13 us
  Pallas kernels: 0 us -> 22.7 us
  matrix products: 18.7 us -> 0 us
  between operations: 0.9 us -> 14.1 us
  starting transfers between devices: 10.2 us -> 0.04 us
    all_to_all x0 -> x1, blocking collectives: none -> 27.4 us  [scatter_sum(): return jnp.sum(lax.all_to_all(blocks, axis, 0, 0, tiled=True), axis=0)]
    all_to_all x2 -> x0, waiting for transfers between devices: 27 us -> none  [scatter_sum(): return jnp.sum(lax.all_to_all(blocks, axis, 0, 0, tiled=True), axis=0)]
    pallas_call x0 -> x8, Pallas kernels: none -> 22.7 us  [call(): pl.pallas_call(kernel, name=name, out_shape=[jax.ShapeDtypeStruct(shape,...]
    dot_general x3 -> x0, matrix products: 18.7 us -> none  [the longest x1 9.55 us: on_device(): lax.dot_general(dscore, embeddings, (((0,), (0,)), ((), ())), precision=l...]
    reduce_sum x15 -> x0, other arithmetic: 12.9 us -> none  [the longest x1 3.19 us: on_device(): jnp.sum(scaled * dg1[None, :], axis=1)]
    all_to_all x2 -> x0, starting transfers between devices: 10.2 us -> none  [scatter_sum(): return jnp.sum(lax.all_to_all(blocks, axis, 0, 0, tiled=True), axis=0)]
    reduce_max x7 -> x0, other arithmetic: 8.57 us -> none  [the longest x2 5.38 us: on_device(): peak = jnp.max(moved, axis=0)]
    mul x1 -> x0, other arithmetic: 5.48 us -> none  [on_device(): INV_EPS * (plan * (grads - factor * dg2[None, :]) - second * df2[:, None]...]
  transfers between devices with their start and end apart: 2 -> 1, of which waited for: 2 -> 1; matrix products, arithmetic and copies ran while one was open for 5% -> 0% of each run, Pallas kernels for 0% -> 0%
where the time goes in v2:
time: 190 us
  blocking collectives  144 us (76%)
  Pallas kernels  22.7 us (12%)
  between operations  14.1 us (7%)
  local copies, waits for them, and re-layouts  5.78 us (3%)
  waiting for transfers between devices  2.13 us (1%)
    all_to_all x7, blocking collectives, to_all(): return lax.all_to_all(copies, axis, 0, 0, tiled=True)  117 us
    all_to_all x1, blocking collectives, scatter_sum(): return jnp.sum(lax.all_to_all(blocks, axis, 0, 0, tiled=True), axis=0)  27.4 us
    pallas_call x8, Pallas kernels, call(): pl.pallas_call(kernel, name=name, out_shape=[jax.ShapeDtypeStruct(shape,...  22.7 us
    unnamed x9, local copies, waits for them, and re-layouts  5.42 us
  transfers between devices with their start and end apart: 1, of which 1 were waited for; matrix products, arithmetic and copies ran while one was open for 0% of the time, Pallas kernels for 0%

profile of v2, /device:TPU:6, one launch (start us, length us, event | category | flops | bytes accessed | tf_op | source)
XLA Modules:
  0.0 189.5 jit_solution(491150710624022725)
XLA Ops:
  7.2 0.0 reduce-scatter.2.cloned.1.call-start
  7.2 0.0 copy-start
  7.2 1.2 copy-done
  8.4 0.0 copy-start.2
  8.4 1.6 copy-done.2
  10.0 0.0 copy-start.3
  10.0 0.9 copy-done.3
  11.0 4.4 %scores.1 = (f32[512,2048]{1,0:T(8,128)S(1)}, bf16[512,2048]{1,0:T(8,128)(2,1)S(1)}, f32[1,2048]{1,0:T(1,128)S(1)}) custom-call(f32[2048,128]{1,0:T(8,128)S(1)} %copy-done, f32[512,128]{1,0:T(8,128)S(1)} %copy-done.3, bf16[2048,512]{1,0:T(8,128)(2,1)S(1)} %copy-done.2), custom_call_target="tpu_custom_call" | custom-call | tf_op jit(solution)/shard_map/scores/pallas_call | solution.py:333
  15.4 9.9 %all_to_all.40.parts = f32[8,1,2048]{2,1,0:T(1,128)S(1)} all-to-all(f32[8,1,2048]{2,1,0:T(1,128)S(1)} %broadcast_in_dim.27), channel_id=1, replica_groups=mesh['comm'=8,'node'=64] {'comm'}, dimensions={0} | all-to-all | bytes 131072 | tf_op jit(solution)/shard_map/all_to_all | solution.py:24
  25.3 1.3 col_lse.1
  26.6 0.1 broadcast_in_dim.57
  26.7 34.0 %all_to_all.41.refs_1_ = f32[64,1,512]{2,1,0:T(1,128)S(1)} all-to-all(f32[64,1,512]{2,1,0:T(1,128)S(1)} %broadcast_in_dim.57), channel_id=1, replica_groups=mesh['comm'=8,'node'=64] {'node'}, dimensions={0} | all-to-all | bytes 262144 | tf_op jit(solution)/shard_map/all_to_all | solution.py:24
  60.7 3.2 %row_lse.1 = (f32[1,512]{1,0:T(1,128)S(1)}, f32[1,2048]{1,0:T(1,128)S(1)}) custom-call(f32[512,2048]{1,0:T(8,128)S(1)} %get-tuple-element.19.logits.refs_0_, f32[64,1,512]{2,1,0:T(1,128)S(1)} %all_to_all.41.refs_1_), custom_call_target="tpu_custom_call" | custom-call | tf_op jit(solution)/shard_map/row_lse/pallas_call | solution.py:333
  63.9 8.0 %all_to_all.42.parts = f32[8,1,2048]{2,1,0:T(1,128)S(1)} all-to-all(f32[8,1,2048]{2,1,0:T(1,128)S(1)} %broadcast_in_dim.59), channel_id=1, replica_groups=mesh['comm'=8,'node'=64] {'comm'}, dimensions={0} | all-to-all | bytes 131072 | tf_op jit(solution)/shard_map/all_to_all | solution.py:24
  71.9 1.6 col_lse_mean.1
  73.6 0.1 broadcast_in_dim.60
  73.7 27.4 %all_to_all.43.refs_2_ = f32[64,2,512]{2,1,0:T(2,128)S(1)} all-to-all(f32[64,2,512]{2,1,0:T(2,128)S(1)} %broadcast_in_dim.60), channel_id=1, replica_groups=mesh['comm'=8,'node'=64] {'node'}, dimensions={0} | all-to-all | bytes 524288 | tf_op jit(solution)/shard_map/all_to_all | solution.py:24
  101.0 2.0 %df2.1 = (f32[512,2048]{1,0:T(8,128)S(1)}, f32[1,2048]{1,0:T(1,128)S(1)}) custom-call(f32[512,2048]{1,0:T(8,128)S(1)} %get-tuple-element.19.logits.refs_0_, f32[1,2048]{1,0:T(1,128)S(1)} %get-tuple-element.26.refs_1_.f2, f32[64,2,512]{2,1,0:T(2,128)S(1)} %all_to_all.43.refs_2_, bf16[512,2048]{1,0:T(8,128)(2,1)S(1)} %get-tuple-element.25.grads.refs_3_), custom_call_target="tpu_custom_call" | custom-call | tf_op jit(solution)/shard_map/df2/pallas_call | solution.py:333
  103.1 8.0 %all_to_all.44.parts = f32[8,1,2048]{2,1,0:T(1,128)S(1)} all-to-all(f32[8,1,2048]{2,1,0:T(1,128)S(1)} %broadcast_in_dim.62), channel_id=1, replica_groups=mesh['comm'=8,'node'=64] {'comm'}, dimensions={0} | all-to-all | bytes 131072 | tf_op jit(solution)/shard_map/all_to_all | solution.py:24
  111.1 1.4 dg1.1
  112.5 0.1 broadcast_in_dim.64
  112.6 21.4 %all_to_all.45.refs_3_ = f32[64,1,512]{2,1,0:T(1,128)S(1)} all-to-all(f32[64,1,512]{2,1,0:T(1,128)S(1)} %broadcast_in_dim.64), channel_id=1, replica_groups=mesh['comm'=8,'node'=64] {'node'}, dimensions={0} | all-to-all | bytes 262144 | tf_op jit(solution)/shard_map/all_to_all | solution.py:24
  134.0 0.0 copy-start.1
  134.0 2.3 %df1.1 = (f32[512,2048]{1,0:T(8,128)S(1)}, f32[1,2048]{1,0:T(1,128)S(1)}) custom-call(f32[512,2048]{1,0:T(8,128)S(1)} %get-tuple-element.19.logits.refs_0_, f32[1,2048]{1,0:T(1,128)S(1)} %get-tuple-element.21.refs_1_.f1, f32[1,512]{1,0:T(1,128)S(1)} %get-tuple-element.23.g1.refs_2_, f32[64,1,512]{2,1,0:T(1,128)S(1)} %all_to_all.45.refs_3_, ...), custom_call_target="tpu_custom_call" | custom-call | tf_op jit(solution)/shard_map/df1/pallas_call | solution.py:333
  136.4 8.0 %all_to_all.46.parts = f32[8,1,2048]{2,1,0:T(1,128)S(1)} all-to-all(f32[8,1,2048]{2,1,0:T(1,128)S(1)} %broadcast_in_dim.66), channel_id=1, replica_groups=mesh['comm'=8,'node'=64] {'comm'}, dimensions={0} | all-to-all | bytes 131072 | tf_op jit(solution)/shard_map/all_to_all | solution.py:24
  144.4 0.0 copy-done.1
  144.4 6.5 %grads.3 = (f32[128,2048]{1,0:T(8,128)}, f32[512,128]{1,0:T(8,128)S(1)}) custom-call(f32[512,2048]{1,0:T(8,128)S(1)} %get-tuple-element.19.logits.refs_0_, f32[1,2048]{1,0:T(1,128)S(1)} %get-tuple-element.21.refs_1_.f1, f32[8,1,2048]{2,1,0:T(1,128)S(1)} %all_to_all.46.parts, f32[512,2048]{1,0:T(8,128)S(1)} %get-tuple-element.33.score, ...), custom_call_target="tpu_custom_call" | custom-call | tf_op jit(solution)/shard_map/grads/pallas_call | solution.py:333
  150.8 0.0 reduce-scatter.2.cloned.1.call-update
  150.9 27.4 %all_to_all.47 = f32[64,8,128]{2,1,0:T(8,128)S(1)} all-to-all(f32[64,8,128]{2,1,0:T(8,128)S(1)} %bitcast.8), channel_id=1, replica_groups=mesh['comm'=8,'node'=64] {'node'}, dimensions={0} | all-to-all | bytes 524288 | tf_op jit(solution)/shard_map/all_to_all | solution.py:30
  178.2 0.7 reduce_sum.9
  178.9 2.1 %reduce-scatter.2.cloned.1.call-done = f32[256,128]{0,1:T(8,128)} async-done(((f32[2048,128]{0,1:T(8,128)}), f32[256,128]{0,1:T(8,128)}) %reduce-scatter.2.cloned.1.call-update) | async-done | bytes 131088 | tf_op jit(solution)/shard_map/reduce_scatter | solution.py:393
  181.0 1.7 copy.5
  (4 shorter events, 0.1 us)
Async XLA Ops:
  7.2 173.9 %reduce-scatter.2.cloned.1.call-start = ((), (), s32[]{:S(2)}) async-start(), calls=%async_computation.9 | async-start | bytes 1179648 | tf_op jit(solution)/shard_map/reduce_scatter | solution.py:393
  7.2 1.2 copy-start
  8.4 1.6 copy-start.2
  10.0 0.9 copy-start.3
  134.0 10.4 %copy-start.1 = (f32[2048,128]{1,0:T(8,128)S(1)}, f32[2048,128]{1,0:T(8,128)}, u32[]{:S(2)}) copy-start(f32[2048,128]{1,0:T(8,128)} %emb.3) | copy-start | bytes 3145732
Sparse Core Ops, SparseCore 0:
  151.0 29.9 reduce-scatter.1

commit v3 on v2

v3 whole, which is shorter than its diff:
```python
import math

import jax
import jax.numpy as jnp
from jax import lax
from jax.experimental import pallas as pl
from jax.experimental.pallas import tpu as pltpu
from jax.sharding import Mesh
from jax.sharding import PartitionSpec as P

INV_EPS = 20.0
LOG2E = 1.0 / math.log(2.0)
LANES = 128
WIDE = 256
SPAN = 4
F32 = jnp.float32
BF16 = jnp.bfloat16
NT = (((1,), (1,)), ((), ()))
EVERY = slice(None)


def to_all(values, axis):
    count = lax.axis_size(axis)
    copies = jnp.broadcast_to(values[None], (count,) + values.shape)
    return lax.all_to_all(copies, axis, 0, 0, tiled=True)


def scatter_sum(blocks, axis):
    return jnp.sum(lax.all_to_all(blocks, axis, 0, 0, tiled=True), axis=0)


def split(x, pieces):
    out = []
    for _ in range(pieces):
        piece = x.astype(BF16)
        out.append(piece)
        x = x - piece.astype(F32)
    return out


def times(left, right):
    hi, low = split(right, 2)
    both = jnp.dot(jnp.concatenate(left, axis=0), hi, preferred_element_type=F32)
    size = left[0].shape[0]
    return both[:size] + both[size:] + jnp.dot(left[0], low, preferred_element_type=F32)


def down(row):
    return jnp.transpose(jnp.broadcast_to(row, (LANES, row.shape[1])))


def tile_rows(at, tall):
    return pl.ds(pl.multiple_of(at * tall, tall), tall)


def lanes_of(ref, rows, tile):
    return ref[rows, tile * LANES : (tile + 1) * LANES]


def add_parts(parts):
    values = [parts[k] for k in range(parts.shape[0])]
    while len(values) > 1:
        values = [a + b for a, b in zip(values[::2], values[1::2])]
    return values[0]


def merge_parts(parts):
    count = parts.shape[0]
    peak = parts[0, 0:1, :]
    for k in range(1, count):
        peak = jnp.maximum(peak, parts[k, 0:1, :])
    mass = jnp.zeros(peak.shape, F32)
    mean = jnp.zeros(peak.shape, F32)
    for k in range(count):
        share = jnp.exp2(parts[k, 0:1, :] - peak)
        mass = mass + share
        if parts.shape[1] == 2:
            mean = mean + share * parts[k, 1:2, :]
    total = peak + jnp.log2(mass)
    return total if parts.shape[1] == 1 else (total, mean / mass)


def scores_kernel(
    emb, proto, grads,
    logits, turned, row_out, e_in, p_in, g_in, sems,
):
    chunks = 4
    size = emb.shape[0] // chunks
    get_p = pltpu.make_async_copy(proto, p_in, sems.at[0])
    get_p.start()
    get_e = []
    for k in range(chunks):
        rows = pl.ds(k * size, size)
        get_e.append(pltpu.make_async_copy(emb.at[rows], e_in.at[rows], sems.at[1 + k]))
        get_e[k].start()
    get_g = pltpu.make_async_copy(grads, g_in, sems.at[1 + chunks])
    get_g.start()
    get_p.wait()
    hi, mid, low = split(p_in[...] * (INV_EPS * LOG2E), 3)
    left = jnp.concatenate([hi, hi, hi, mid, mid, low], axis=1)
    for at in range(0, emb.shape[0], 2 * size):
        get_e[at // size].wait()
        get_e[at // size + 1].wait()
        lanes = slice(at, at + 2 * size)
        hi, mid, low = split(e_in[lanes, :], 3)
        right = jnp.concatenate([hi, mid, low, hi, mid, hi], axis=1)
        tile = lax.dot_general(left, right, NT, preferred_element_type=F32)
        logits[:, lanes] = tile
        peak = jnp.max(tile, axis=0, keepdims=True)
        mass = jnp.sum(jnp.exp2(tile - peak), axis=0, keepdims=True)
        row_out[:, lanes] = peak + jnp.log2(mass)
    eye = (
        lax.broadcasted_iota(jnp.int32, (WIDE, WIDE), 0)
        == lax.broadcasted_iota(jnp.int32, (WIDE, WIDE), 1)
    ).astype(F32).astype(BF16)
    get_g.wait()
    for at in range(0, grads.shape[1], WIDE):
        turned[at : at + WIDE, :] = lax.dot_general(
            eye, g_in[:, at : at + WIDE], NT, preferred_element_type=F32
        ).astype(BF16)


def col_kernel(logits, parts, f1, lse_out, shifts, peaks, masses):
    tiles = logits.shape[1] // LANES
    f1[...] = -merge_parts(parts)
    shifts[...] = jnp.broadcast_to(f1[...], shifts.shape)

    def step(at, _):
        rows = tile_rows(at, 8)
        moved = [lanes_of(logits, rows, k) + lanes_of(shifts, EVERY, k) for k in range(tiles)]
        peak = moved[0]
        for part in moved[1:]:
            peak = jnp.maximum(peak, part)
        mass = jnp.exp2(moved[0] - peak)
        for part in moved[1:]:
            mass = mass + jnp.exp2(part - peak)
        peaks[rows, :] = peak
        masses[rows, :] = mass
        return 0

    lax.fori_loop(0, logits.shape[0] // 8, step, 0, unroll=4)
    peak_t = jnp.transpose(peaks[...])
    peak = jnp.max(peak_t, axis=0, keepdims=True)
    mass = jnp.sum(jnp.transpose(masses[...]) * jnp.exp2(peak_t - peak), axis=0, keepdims=True)
    lse_out[...] = peak + jnp.log2(mass)


def merge_kernel(parts, out):
    total, mean = merge_parts(parts)
    out[0:1, :] = total
    out[1:2, :] = mean


def col_mean_kernel(logits, parts, grads, f2, out, shifts, peaks, masses, means):
    tiles = logits.shape[1] // LANES
    f2[...] = -merge_parts(parts)
    shifts[...] = jnp.broadcast_to(f2[...], shifts.shape)

    def step(at, _):
        rows = tile_rows(at, 16)
        peak = lanes_of(logits, rows, 0) + lanes_of(shifts, EVERY, 0)
        for k in range(1, tiles):
            peak = jnp.maximum(peak, lanes_of(logits, rows, k) + lanes_of(shifts, EVERY, k))
        mass = jnp.zeros((16, LANES), F32)
        mean = jnp.zeros((16, LANES), F32)
        for k in range(tiles):
            term = jnp.exp2(lanes_of(logits, rows, k) + lanes_of(shifts, EVERY, k) - peak)
            mass = mass + term
            mean = mean + term * lanes_of(grads, rows, k).astype(F32)
        peaks[rows, :] = peak
        masses[rows, :] = mass
        means[rows, :] = mean
        return 0

    lax.fori_loop(0, logits.shape[0] // 16, step, 0, unroll=2)
    peak_t = jnp.transpose(peaks[...])
    peak = jnp.max(peak_t, axis=0, keepdims=True)
    share = jnp.exp2(peak_t - peak)
    mass = jnp.sum(jnp.transpose(masses[...]) * share, axis=0, keepdims=True)
    mean = jnp.sum(jnp.transpose(means[...]) * share, axis=0, keepdims=True)
    out[0:1, :] = peak + jnp.log2(mass)
    out[1:2, :] = mean / mass


def spans(ref, size):
    tiles = ref.shape[1] // LANES
    for at in range(0, tiles, size):
        yield [slice(k * LANES, (k + 1) * LANES) for k in range(at, at + size)]


def row_kernel(log_mass, logits, parts, g1, lse_out, shifts):
    g1[...] = log_mass - merge_parts(parts)
    shifts[...] = down(g1[...])
    count = logits.shape[0] // 8
    for lanes in spans(logits, SPAN):

        def highest(at, peak):
            rows = tile_rows(at, 8)
            move = shifts[rows, :]
            return [jnp.maximum(p, logits[rows, s] + move) for p, s in zip(peak, lanes)]

        peak = lax.fori_loop(
            0, count, highest, [jnp.full((8, LANES), -jnp.inf, F32)] * SPAN, unroll=count
        )
        peak = [jnp.max(part, axis=0, keepdims=True) for part in peak]

        def add(at, mass):
            rows = tile_rows(at, 8)
            move = shifts[rows, :]
            return [
                m + jnp.exp2(logits[rows, s] + move - p) for m, p, s in zip(mass, peak, lanes)
            ]

        mass = lax.fori_loop(0, count, add, [jnp.zeros((8, LANES), F32)] * SPAN, unroll=count)
        for p, m, s in zip(peak, mass, lanes):
            lse_out[:, s] = p + jnp.log2(jnp.sum(m, axis=0, keepdims=True))


def df2_kernel(log_mass, logits, f2, parts, grads, score, out, cols, weights):
    total, mean = merge_parts(parts)
    cols[...] = down(log_mass - total)
    weights[...] = down(mean)
    tall = 16
    count = logits.shape[0] // tall
    for lanes in spans(logits, SPAN):
        moves = [f2[:, s] for s in lanes]

        def add(at, total):
            rows = tile_rows(at, tall)
            move = cols[rows, :]
            weigh = weights[rows, :]
            new = []
            for t, m, s in zip(total, moves, lanes):
                term = jnp.exp2(logits[rows, s] + move + m)
                term = term * (grads[rows, s].astype(F32) - weigh)
                score[rows, s] = term
                new.append(t + term[:8] + term[8:])
            return new

        total = lax.fori_loop(0, count, add, [jnp.zeros((8, LANES), F32)] * SPAN, unroll=count)
        for t, s in zip(total, lanes):
            out[:, s] = jnp.sum(t, axis=0, keepdims=True)


def dg1_kernel(logits, f2, g1, parts, score, rest, out, rows_of, weights, cols, sums):
    tiles = logits.shape[1] // LANES
    rows_of[...] = jnp.broadcast_to(f2[...], rows_of.shape)
    weights[...] = jnp.broadcast_to(add_parts(parts), weights.shape)
    cols[...] = down(g1[...])

    def step(at, _):
        rows = tile_rows(at, 8)
        move = cols[rows, :]
        total = jnp.zeros((8, LANES), F32)
        for k in range(tiles):
            term = jnp.exp2(lanes_of(logits, rows, k) + lanes_of(rows_of, EVERY, k) + move)
            term = term * lanes_of(weights, EVERY, k)
            rest[rows, k * LANES : (k + 1) * LANES] = lanes_of(score, rows, k) - term
            total = total + term
        sums[rows, :] = total
        return 0

    lax.fori_loop(0, logits.shape[0] // 8, step, 0, unroll=4)
    out[...] = -jnp.sum(jnp.transpose(sums[...]), axis=0, keepdims=True)


def proto_term(score, emb):
    width = emb.shape[1]
    s_hi, s_low = split(score, 2)
    e_hi, e_low = split(emb * INV_EPS, 2)
    both = jnp.dot(s_hi, jnp.concatenate([e_hi, e_low], axis=1), preferred_element_type=F32)
    low = jnp.dot(s_low, e_hi, preferred_element_type=F32)
    return both[:, :width] + both[:, width:] + low


def df1_kernel(log_mass, logits, f1, g1, parts, score, rest, out, cols, weights):
    cols[...] = down(g1[...] - log_mass)
    weights[...] = down(add_parts(parts))
    count = logits.shape[0] // 8
    for lanes in spans(logits, SPAN):
        moves = [f1[:, s] for s in lanes]

        def add(at, total):
            rows = tile_rows(at, 8)
            move = cols[rows, :]
            weigh = weights[rows, :]
            new = []
            for t, m, s in zip(total, moves, lanes):
                term = jnp.exp2(logits[rows, s] + move + m) * weigh
                rest[rows, s] = score[rows, s] - term
                new.append(t + term)
            return new

        total = lax.fori_loop(0, count, add, [jnp.zeros((8, LANES), F32)] * SPAN, unroll=count)
        for t, s in zip(total, lanes):
            out[:, s] = -jnp.sum(t, axis=0, keepdims=True)


def proto_kernel(logits, f1, parts, score, emb, dlog, proto_out):
    df1 = add_parts(parts)
    step = 2 * SPAN * LANES
    total = jnp.zeros((logits.shape[0], emb.shape[1]), F32)
    for at in range(0, logits.shape[1], step):
        nodes = slice(at, at + step)
        dlog[:, nodes] = score[:, nodes] - jnp.exp2(logits[:, nodes] + f1[:, nodes]) * df1[:, nodes]
        total = total + proto_term(dlog[:, nodes], emb[nodes, :])
    xs, zs, tall, _ = proto_out.shape
    for x in range(xs):
        for z in range(zs):
            start = (z * xs + x) * tall
            proto_out[x, z] = total[start : start + tall]


def emb_kernel(place, dlog, proto, keep, send):
    turned_p = split(jnp.transpose(proto[...]) * INV_EPS, 2)
    size = keep.shape[2]
    part = times(turned_p, dlog[...])
    for y in range(keep.shape[0]):
        even = part[:, 2 * y * size : (2 * y + 1) * size]
        odd = part[:, (2 * y + 1) * size : (2 * y + 2) * size]

        @pl.when(place[1] == 0)
        def _():
            keep[y] = even
            send[y] = odd

        @pl.when(place[1] != 0)
        def _():
            keep[y] = odd
            send[y] = even


def pair_kernel(place, keep, other, *outs):
    for k, out in enumerate(outs):
        y = place[0] ^ k
        out[...] = keep[y] + other[y]


def last_kernel(*refs):
    *parts, out = refs
    total = parts[0][...]
    for part in parts[1:]:
        total = total + part[...]
    out[...] = jnp.transpose(total)


def call(kernel, name, outs, scratch, args, in_places=(), out_places=()):
    vmem = pl.BlockSpec(memory_space=pltpu.VMEM)
    place = lambda places, k: pl.BlockSpec(memory_space=places[k]) if k in places else vmem
    return pl.pallas_call(
        kernel,
        name=name,
        out_shape=[
            dict(out_places)[k](shape, dtype)
            if k in dict(out_places)
            else jax.ShapeDtypeStruct(shape, dtype)
            for k, (shape, dtype) in enumerate(outs)
        ],
        in_specs=[place(dict(in_places), k) for k in range(len(args))],
        out_specs=[place(dict(out_places), k) for k in range(len(outs))],
        scratch_shapes=[
            s if not isinstance(s, tuple) else pltpu.VMEM(s, F32) for s in scratch
        ],
        compiler_params=pltpu.CompilerParams(vmem_limit_bytes=24 * 2**20),
    )(*args)


def on_device(embeddings, prototypes, plan_grad):
    rows, width = embeddings.shape
    local = prototypes.shape[0]
    ys = lax.axis_size("y")
    comms = ys * lax.axis_size("core")
    xs = lax.axis_size("x")
    zs = lax.axis_size("z")
    per_proto = (rows * zs * xs) / (local * comms)
    log_mass = math.log2(per_proto)
    full = ((local, rows), F32)
    row = ((1, rows), F32)
    col = ((1, local), F32)
    two = ((2, local), F32)
    tall = (local, LANES)
    block = ((width, rows // comms), F32)
    blocks = ((ys,) + block[0], F32)
    node = ("z", "x")
    comm = ("y", "core")
    hbm = pltpu.HBM
    place = jnp.stack([lax.axis_index("y"), lax.axis_index("core")])

    logits, grads, here = call(
        scores_kernel, "scores", [full, ((local, rows), BF16), row],
        [(rows, width), (local, width), pltpu.VMEM((rows, local), BF16),
         pltpu.SemaphoreType.DMA((6,))],
        [pltpu.with_memory_space_constraint(x, hbm)
         for x in (embeddings, prototypes, plan_grad)],
        {0: hbm, 1: hbm, 2: hbm},
    )
    here, place = lax.optimization_barrier((here, place))
    f1, here = call(
        col_kernel, "col_lse", [row, col], [(8, rows), tall, tall], [logits, to_all(here, comm)]
    )
    g1, here = call(
        lambda *refs: row_kernel(log_mass, *refs), "row_lse", [col, row], [tall],
        [logits, to_all(here, node)],
    )
    f2, here = call(
        col_mean_kernel, "col_lse_mean", [row, two],
        [(16, rows), tall, tall, tall], [logits, to_all(here, comm), grads],
    )
    (here,) = call(merge_kernel, "merge_x", [two], [], [to_all(here, "x")])
    score, here = call(
        lambda *refs: df2_kernel(log_mass, *refs), "df2", [full, row], [tall, tall],
        [logits, f2, to_all(here, "z"), grads],
    )
    score, here = call(
        dg1_kernel, "dg1", [full, col], [(8, rows), (8, rows), tall, tall],
        [logits, f2, g1, to_all(here, comm), score],
    )
    score, here = call(
        lambda *refs: df1_kernel(log_mass, *refs), "df1", [full, row], [tall, tall],
        [logits, f1, g1, to_all(here, node), score],
    )
    dlog, proto_part = call(
        proto_kernel, "proto", [full, ((xs, zs, local // (xs * zs), width), F32)], [],
        [logits, f1, to_all(here, comm), score, embeddings],
    )
    grad_proto = scatter_sum(scatter_sum(proto_part, "x"), "z")
    keep, send = call(
        emb_kernel, "emb", [blocks, blocks], [], [place, dlog, prototypes], {0: pltpu.SMEM}
    )
    other = lax.ppermute(send, "core", [(0, 1), (1, 0)])
    parts = call(
        pair_kernel, "emb_pair", [block] * ys, [], [place, keep, other], {0: pltpu.SMEM}
    )
    parts = list(parts)
    for k in range(1, ys):
        parts[k] = lax.ppermute(parts[k], "y", [(y, y ^ k) for y in range(ys)])
    (grad_emb,) = call(last_kernel, "emb_last", [(block[0][::-1], F32)], [], parts)
    return grad_emb, grad_proto


def solution(mesh):
    split_mesh = Mesh(mesh.devices.reshape(4, 2, 16, 4), ("y", "core", "z", "x"))
    node = ("z", "x")
    comm = ("y", "core")
    in_specs = (P(node, None), P(comm, None), P(node, comm))
    out_specs = (P(node + comm, None), P(comm + node, None))
    return jax.shard_map(
        on_device, mesh=split_mesh, in_specs=in_specs, out_specs=out_specs, check_vma=False
    )
```

time: 190 us -> 164 us (0.86)
  blocking collectives: 144 us -> 123 us
  starting transfers between devices: 0.04 us -> 15.8 us
  between operations: 14.1 us -> 0.83 us
  Pallas kernels: 22.7 us -> 17.1 us
  local copies, waits for them, and re-layouts: 5.78 us -> 0.32 us
    all_to_all x1, blocking collectives: 27.4 us -> 10.3 us  [scatter_sum(): return jnp.sum(lax.all_to_all(blocks, axis, 0, 0, tiled=True), axis=0)]
    ppermute x0 -> x4, starting transfers between devices: none -> 12.3 us  [the longest x3 10.4 us: on_device(): parts[k] = lax.ppermute(parts[k], 'y', [(y, y ^ k) for y in range(ys)])]
    pallas_call x8 -> x12, Pallas kernels: 22.7 us -> 17.1 us  [call(): pl.pallas_call(kernel, name=name, out_shape=[dict(out_places)[k](shape, d...]
    unnamed x9 -> x4, local copies, waits for them, and re-layouts: 5.42 us -> 0.01 us
    all_to_all x7 -> x8, blocking collectives: 117 us -> 113 us  [to_all(): return lax.all_to_all(copies, axis, 0, 0, tiled=True)]
    all_to_all x0 -> x1, starting transfers between devices: none -> 3.5 us  [scatter_sum(): return jnp.sum(lax.all_to_all(blocks, axis, 0, 0, tiled=True), axis=0)]
    reduce_scatter x1 -> x0, waiting for transfers between devices: 2.11 us -> none  [on_device(): lax.psum_scatter(emb_part.T, 'comm', scatter_dimension=0, tiled=True)]
    ppermute x0 -> x4, waiting for transfers between devices: none -> 1.92 us  [the longest x3 1.92 us: on_device(): parts[k] = lax.ppermute(parts[k], 'y', [(y, y ^ k) for y in range(ys)])]
  transfers between devices with their start and end apart: 1 -> 5, of which waited for: 1 -> 2; matrix products, arithmetic and copies ran while one was open for 0% -> 1% of each run, Pallas kernels for 0% -> 0%
where the time goes in v3:
time: 164 us; the launch traced here: 162 us
  blocking collectives  123 us (75%)
  Pallas kernels  17.1 us (10%)
  starting transfers between devices  15.8 us (10%)
  waiting for transfers between devices  3.47 us (2%)
    all_to_all x8, blocking collectives, to_all(): return lax.all_to_all(copies, axis, 0, 0, tiled=True)  113 us
    pallas_call x12, Pallas kernels, call(): pl.pallas_call(kernel, name=name, out_shape=[dict(out_places)[k](shape, d...  17.1 us
    ppermute x3, starting transfers between devices, on_device(): parts[k] = lax.ppermute(parts[k], 'y', [(y, y ^ k) for y in range(ys)])  10.4 us
    all_to_all x1, blocking collectives, scatter_sum(): return jnp.sum(lax.all_to_all(blocks, axis, 0, 0, tiled=True), axis=0)  10.3 us
    all_to_all x1, starting transfers between devices, scatter_sum(): return jnp.sum(lax.all_to_all(blocks, axis, 0, 0, tiled=True), axis=0)  3.5 us
  transfers between devices with their start and end apart: 5, of which 2 were waited for; matrix products, arithmetic and copies ran while one was open for 1% of the time, Pallas kernels for 0%

profile of v3, /device:TPU:6, one launch (start us, length us, event | category | flops | bytes accessed | tf_op | source)
XLA Modules:
  0.0 162.0 jit_solution(18038769012298023223)
XLA Ops:
  0.6 0.1 pad_add_fusion.place
  0.7 4.6 %scores.1 = (f32[512,2048]{1,0:T(8,128)S(1)}, bf16[512,2048]{1,0:T(8,128)(2,1)S(1)}, f32[1,2048]{1,0:T(1,128)S(1)}) custom-call(f32[2048,128]{1,0:T(8,128)} %emb.4, f32[512,128]{1,0:T(8,128)} %proto.5, bf16[2048,512]{1,0:T(8,128)(2,1)} %grads.1), custom_call_target="tpu_custom_call" | custom-call | tf_op jit(solution)/shard_map/scores/pallas_call | solution.py:350
  5.3 9.9 %all_to_all.50.parts = f32[8,1,2048]{2,1,0:T(1,128)S(1)} all-to-all(f32[8,1,2048]{2,1,0:T(1,128)S(1)} %broadcast_in_dim.29), channel_id=1, replica_groups=mesh['y'=4,'core'=2,'z'=16,'x'=4] {'y','core'}, dimensions={0} | all-to-all | bytes 131072 | tf_op jit(solution)/shard_map/all_to_all | solution.py:25
  15.2 1.4 col_lse.1
  16.6 0.1 broadcast_in_dim.31
  16.7 34.0 %all_to_all.51.refs_1_ = f32[64,1,512]{2,1,0:T(1,128)S(1)} all-to-all(f32[64,1,512]{2,1,0:T(1,128)S(1)} %broadcast_in_dim.31), channel_id=1, replica_groups=mesh['y'=4,'core'=2,'z'=16,'x'=4] {'z','x'}, dimensions={0} | all-to-all | bytes 262144 | tf_op jit(solution)/shard_map/all_to_all | solution.py:25
  50.7 1.1 row_lse.1
  51.8 8.0 %all_to_all.52.parts = f32[8,1,2048]{2,1,0:T(1,128)S(1)} all-to-all(f32[8,1,2048]{2,1,0:T(1,128)S(1)} %broadcast_in_dim.65), channel_id=1, replica_groups=mesh['y'=4,'core'=2,'z'=16,'x'=4] {'y','core'}, dimensions={0} | all-to-all | bytes 131072 | tf_op jit(solution)/shard_map/all_to_all | solution.py:25
  59.8 1.7 %col_lse_mean.1 = (f32[1,2048]{1,0:T(1,128)S(1)}, f32[2,512]{1,0:T(2,128)S(1)}) custom-call(f32[512,2048]{1,0:T(8,128)S(1)} %get-tuple-element.29.logits.refs_0_, f32[8,1,2048]{2,1,0:T(1,128)S(1)} %all_to_all.52.parts, bf16[512,2048]{1,0:T(8,128)(2,1)S(1)} %get-tuple-element.35.grads.refs_3_), custom_call_target="tpu_custom_call" | custom-call | tf_op jit(solution)/shard_map/col_lse_mean/pallas_call | solution.py:350
  61.5 8.0 %all_to_all.53.parts = f32[4,2,512]{2,1,0:T(2,128)S(1)} all-to-all(f32[4,2,512]{2,1,0:T(2,128)S(1)} %broadcast_in_dim.66), channel_id=1, replica_groups=mesh['y'=4,'core'=2,'z'=16,'x'=4] {'x'}, dimensions={0} | all-to-all | bytes 32768 | tf_op jit(solution)/shard_map/all_to_all | solution.py:25
  69.6 15.4 %all_to_all.54.refs_2_ = f32[16,2,512]{2,1,0:T(2,128)S(1)} all-to-all(f32[16,2,512]{2,1,0:T(2,128)S(1)} %broadcast_in_dim.67), channel_id=1, replica_groups=mesh['y'=4,'core'=2,'z'=16,'x'=4] {'z'}, dimensions={0} | all-to-all | bytes 131072 | tf_op jit(solution)/shard_map/all_to_all | solution.py:25
  85.0 1.2 df2.1
  86.3 8.0 %all_to_all.55.parts = f32[8,1,2048]{2,1,0:T(1,128)S(1)} all-to-all(f32[8,1,2048]{2,1,0:T(1,128)S(1)} %broadcast_in_dim.69), channel_id=1, replica_groups=mesh['y'=4,'core'=2,'z'=16,'x'=4] {'y','core'}, dimensions={0} | all-to-all | bytes 131072 | tf_op jit(solution)/shard_map/all_to_all | solution.py:25
  94.3 1.4 dg1.1
  95.8 0.1 broadcast_in_dim.71
  95.8 21.4 %all_to_all.56.refs_3_ = f32[64,1,512]{2,1,0:T(1,128)S(1)} all-to-all(f32[64,1,512]{2,1,0:T(1,128)S(1)} %broadcast_in_dim.71), channel_id=1, replica_groups=mesh['y'=4,'core'=2,'z'=16,'x'=4] {'z','x'}, dimensions={0} | all-to-all | bytes 262144 | tf_op jit(solution)/shard_map/all_to_all | solution.py:25
  117.3 0.0 copy-start
  117.3 1.1 df1.1
  118.5 8.0 %all_to_all.57.parts = f32[8,1,2048]{2,1,0:T(1,128)S(1)} all-to-all(f32[8,1,2048]{2,1,0:T(1,128)S(1)} %broadcast_in_dim.73), channel_id=1, replica_groups=mesh['y'=4,'core'=2,'z'=16,'x'=4] {'y','core'}, dimensions={0} | all-to-all | bytes 131072 | tf_op jit(solution)/shard_map/all_to_all | solution.py:25
  126.5 0.0 copy-done
  126.5 0.0 copy-start.1
  126.5 1.3 proto.4
  127.8 0.0 copy-done.1
  127.8 1.9 %emb.5 = (f32[4,128,256]{2,1,0:T(8,128)S(1)}, f32[4,128,256]{2,1,0:T(8,128)S(1)}) custom-call(s32[2]{0:T(128)S(1)} %pad_add_fusion.place, f32[512,2048]{1,0:T(8,128)S(1)} %get-tuple-element.44.dlog, f32[512,128]{1,0:T(8,128)S(1)} %copy-done.1), custom_call_target="tpu_custom_call" | custom-call | tf_op jit(solution)/shard_map/emb/pallas_call | solution.py:350
  129.7 1.9 %collective-permute-start = (f32[4,128,256]{2,1,0:T(8,128)S(1)}, f32[4,128,256]{2,1,0:T(8,128)S(1)}, u32[]{:S(2)}, u32[]{:S(2)}) collective-permute-start(f32[4,128,256]{2,1,0:T(8,128)S(1)} %get-tuple-element.46), channel_id=1, source_target_pairs={{0,64},{64,0},{1,65},{65,1},{2,66},{66,2},{3,67},{67,3},{4,68},{68... | collective-permute-start | bytes 1572872 | tf_op jit(solution)/shard_map/ppermute | solution.py:430
  131.6 10.3 %all_to_all.58 = f32[4,16,8,128]{3,2,1,0:T(8,128)S(1)} all-to-all(f32[4,16,8,128]{3,2,1,0:T(8,128)S(1)} %get-tuple-element.51), channel_id=1, replica_groups=mesh['y'=4,'core'=2,'z'=16,'x'=4] {'x'}, dimensions={0} | all-to-all | bytes 524288 | tf_op jit(solution)/shard_map/all_to_all | solution.py:29
  141.9 0.6 reduce_sum.18
  142.6 3.5 %all-to-all-start.9 = ((f32[16,8,128]{2,1,0:T(8,128)}), f32[16,8,128]{2,1,0:T(8,128)S(1)}, u32[]{:S(2)}, u32[]{:S(2)}) async-start(f32[16,8,128]{2,1,0:T(8,128)} %reduce_sum.18), calls=%async_computation.9 | async-start | bytes 131072 | tf_op jit(solution)/shard_map/all_to_all | solution.py:29
  146.1 0.0 collective-permute-done.other
  146.1 0.6 emb_pair.1
  146.7 2.5 %collective-permute-start.1 = (f32[128,256]{1,0:T(8,128)S(1)}, f32[128,256]{1,0:T(8,128)S(1)}, u32[]{:S(2)}, u32[]{:S(2)}) collective-permute-start(f32[128,256]{1,0:T(8,128)S(1)} %get-tuple-element.48), channel_id=1, source_target_pairs={{0,128},{128,0},{256,384},{384,256},{1,129},{129,1},{257,385},{385... | collective-permute-start | bytes 393224 | tf_op jit(solution)/shard_map/ppermute | solution.py:436
  149.2 4.0 %collective-permute-start.2 = (f32[128,256]{1,0:T(8,128)S(1)}, f32[128,256]{1,0:T(8,128)S(1)}, u32[]{:S(2)}, u32[]{:S(2)}) collective-permute-start(f32[128,256]{1,0:T(8,128)S(1)} %get-tuple-element.49), channel_id=1, source_target_pairs={{0,256},{128,384},{256,0},{384,128},{1,257},{129,385},{257,1},{385... | collective-permute-start | bytes 393224 | tf_op jit(solution)/shard_map/ppermute | solution.py:436
  153.2 4.0 %collective-permute-start.3 = (f32[128,256]{1,0:T(8,128)S(1)}, f32[128,256]{1,0:T(8,128)S(1)}, u32[]{:S(2)}, u32[]{:S(2)}) collective-permute-start(f32[128,256]{1,0:T(8,128)S(1)} %get-tuple-element.50), channel_id=1, source_target_pairs={{0,384},{128,256},{256,128},{384,0},{1,385},{129,257},{257,129},{3... | collective-permute-start | bytes 393224 | tf_op jit(solution)/shard_map/ppermute | solution.py:436
  157.2 1.6 all-to-all-done.9
  158.7 0.6 reduce_sum.19
  159.3 0.0 collective-permute-done.1.refs_1_
  159.3 0.0 collective-permute-done.2.refs_2_
  159.3 1.9 %collective-permute-done.3.refs_3_ = f32[128,256]{1,0:T(8,128)S(1)} collective-permute-done((f32[128,256]{1,0:T(8,128)S(1)}, f32[128,256]{1,0:T(8,128)S(1)}, u32[]{:S(2)}, u32[]{:S(2)}) %collective-permute-start.3) | collective-permute-done | bytes 131104 | tf_op jit(solution)/shard_map/ppermute | solution.py:436
  161.2 0.8 emb_last.1
  (7 shorter events, 0.2 us)
Async XLA Ops:
  117.3 9.2 %copy-start = (f32[2048,128]{1,0:T(8,128)S(1)}, f32[2048,128]{1,0:T(8,128)}, u32[]{:S(2)}) copy-start(f32[2048,128]{1,0:T(8,128)} %emb.4) | copy-start | bytes 3145732
  126.5 1.3 copy-start.1
  129.7 16.4 %collective-permute-start = (f32[4,128,256]{2,1,0:T(8,128)S(1)}, f32[4,128,256]{2,1,0:T(8,128)S(1)}, u32[]{:S(2)}, u32[]{:S(2)}) collective-permute-start(f32[4,128,256]{2,1,0:T(8,128)S(1)} %get-tuple-element.46), channel_id=1, source_target_pairs={{0,64},{64,0},{1,65},{65,1},{2,66},{66,2},{3,67},{67,3},{4,68},{68... | collective-permute-start | bytes 1572872 | tf_op jit(solution)/shard_map/ppermute | solution.py:430
  142.6 16.1 %all-to-all-start.9 = ((f32[16,8,128]{2,1,0:T(8,128)}), f32[16,8,128]{2,1,0:T(8,128)S(1)}, u32[]{:S(2)}, u32[]{:S(2)}) async-start(f32[16,8,128]{2,1,0:T(8,128)} %reduce_sum.18), calls=%async_computation.9 | async-start | bytes 131072 | tf_op jit(solution)/shard_map/all_to_all | solution.py:29
  146.7 12.6 %collective-permute-start.1 = (f32[128,256]{1,0:T(8,128)S(1)}, f32[128,256]{1,0:T(8,128)S(1)}, u32[]{:S(2)}, u32[]{:S(2)}) collective-permute-start(f32[128,256]{1,0:T(8,128)S(1)} %get-tuple-element.48), channel_id=1, source_target_pairs={{0,128},{128,0},{256,384},{384,256},{1,129},{129,1},{257,385},{385... | collective-permute-start | bytes 393224 | tf_op jit(solution)/shard_map/ppermute | solution.py:436
  149.2 10.1 %collective-permute-start.2 = (f32[128,256]{1,0:T(8,128)S(1)}, f32[128,256]{1,0:T(8,128)S(1)}, u32[]{:S(2)}, u32[]{:S(2)}) collective-permute-start(f32[128,256]{1,0:T(8,128)S(1)} %get-tuple-element.49), channel_id=1, source_target_pairs={{0,256},{128,384},{256,0},{384,128},{1,257},{129,385},{257,1},{385... | collective-permute-start | bytes 393224 | tf_op jit(solution)/shard_map/ppermute | solution.py:436
  153.2 8.1 %collective-permute-start.3 = (f32[128,256]{1,0:T(8,128)S(1)}, f32[128,256]{1,0:T(8,128)S(1)}, u32[]{:S(2)}, u32[]{:S(2)}) collective-permute-start(f32[128,256]{1,0:T(8,128)S(1)} %get-tuple-element.50), channel_id=1, source_target_pairs={{0,384},{128,256},{256,128},{384,0},{1,385},{129,257},{257,129},{3... | collective-permute-start | bytes 393224 | tf_op jit(solution)/shard_map/ppermute | solution.py:436

commit v4 on v3

--- a/solution.py
+++ b/solution.py
@@ -98,14 +98,16 @@
     get_p.wait()
     hi, mid, low = split(p_in[...] * (INV_EPS * LOG2E), 3)
     left = jnp.concatenate([hi, hi, hi, mid, mid, low], axis=1)
-    for at in range(0, emb.shape[0], 2 * size):
-        get_e[at // size].wait()
-        get_e[at // size + 1].wait()
-        lanes = slice(at, at + 2 * size)
+    for get in get_e:
+        get.wait()
+    for at in range(0, emb.shape[0], size):
+        lanes = slice(at, at + size)
         hi, mid, low = split(e_in[lanes, :], 3)
         right = jnp.concatenate([hi, mid, low, hi, mid, hi], axis=1)
         tile = lax.dot_general(left, right, NT, preferred_element_type=F32)
         logits[:, lanes] = tile
+        if at + size == emb.shape[0]:
+            get_g.wait()
         peak = jnp.max(tile, axis=0, keepdims=True)
         mass = jnp.sum(jnp.exp2(tile - peak), axis=0, keepdims=True)
         row_out[:, lanes] = peak + jnp.log2(mass)
@@ -113,7 +115,6 @@
         lax.broadcasted_iota(jnp.int32, (WIDE, WIDE), 0)
         == lax.broadcasted_iota(jnp.int32, (WIDE, WIDE), 1)
     ).astype(F32).astype(BF16)
-    get_g.wait()
     for at in range(0, grads.shape[1], WIDE):
         turned[at : at + WIDE, :] = lax.dot_general(
             eye, g_in[:, at : at + WIDE], NT, preferred_element_type=F32
@@ -296,42 +297,29 @@
             out[:, s] = -jnp.sum(t, axis=0, keepdims=True)
 
 
-def proto_kernel(logits, f1, parts, score, emb, dlog, proto_out):
+def grads_kernel(place, logits, f1, parts, score, emb, proto, keep, send, proto_out):
     df1 = add_parts(parts)
-    step = 2 * SPAN * LANES
-    total = jnp.zeros((logits.shape[0], emb.shape[1]), F32)
+    turned_p = split(jnp.transpose(proto[...]) * INV_EPS, 2)
+    size = keep.shape[2]
+    step = 4 * size
+    total = jnp.zeros(proto_out.shape, F32)
     for at in range(0, logits.shape[1], step):
         nodes = slice(at, at + step)
-        dlog[:, nodes] = score[:, nodes] - jnp.exp2(logits[:, nodes] + f1[:, nodes]) * df1[:, nodes]
-        total = total + proto_term(dlog[:, nodes], emb[nodes, :])
-    xs, zs, tall, _ = proto_out.shape
-    for x in range(xs):
-        for z in range(zs):
-            start = (z * xs + x) * tall
-            proto_out[x, z] = total[start : start + tall]
-
-
-def emb_kernel(place, dlog, proto, keep, send):
-    turned_p = split(jnp.transpose(proto[...]) * INV_EPS, 2)
-    size = keep.shape[2]
-    part = times(turned_p, dlog[...])
-    for y in range(keep.shape[0]):
-        even = part[:, 2 * y * size : (2 * y + 1) * size]
-        odd = part[:, (2 * y + 1) * size : (2 * y + 2) * size]
-
-        @pl.when(place[1] == 0)
-        def _():
-            keep[y] = even
-            send[y] = odd
-
-        @pl.when(place[1] != 0)
-        def _():
-            keep[y] = odd
-            send[y] = even
-
-
-def pair_kernel(place, keep, other, *outs):
-    for k, out in enumerate(outs):
+        dlog = score[:, nodes] - jnp.exp2(logits[:, nodes] + f1[:, nodes]) * df1[:, nodes]
+        part = times(turned_p, dlog)
+        for k in range(0, step // size, 2):
+            y = (at // size + k) // 2
+            even = part[:, k * size : (k + 1) * size]
+            odd = part[:, (k + 1) * size : (k + 2) * size]
+            first = place[1] == 0
+            keep[y] = jnp.where(first, even, odd)
+            send[y] = jnp.where(first, odd, even)
+        total = total + proto_term(dlog, emb[nodes, :])
+    proto_out[...] = total
+
+
+def pair_kernel(order, place, keep, other, *outs):
+    for k, out in zip(order, outs):
         y = place[0] ^ k
         out[...] = keep[y] + other[y]
 
@@ -419,21 +407,21 @@
         lambda *refs: df1_kernel(log_mass, *refs), "df1", [full, row], [tall, tall],
         [logits, f1, g1, to_all(here, node), score],
     )
-    dlog, proto_part = call(
-        proto_kernel, "proto", [full, ((xs, zs, local // (xs * zs), width), F32)], [],
-        [logits, f1, to_all(here, comm), score, embeddings],
-    )
-    grad_proto = scatter_sum(scatter_sum(proto_part, "x"), "z")
-    keep, send = call(
-        emb_kernel, "emb", [blocks, blocks], [], [place, dlog, prototypes], {0: pltpu.SMEM}
+    keep, send, proto_part = call(
+        grads_kernel, "grads", [blocks, blocks, ((local, width), F32)], [],
+        [place, logits, f1, to_all(here, comm), score, embeddings, prototypes], {0: pltpu.SMEM},
     )
     other = lax.ppermute(send, "core", [(0, 1), (1, 0)])
+    grad_proto = scatter_sum(proto_part.reshape(xs * zs, -1, width), node)
+    order = (2, 1, 3, 0)
     parts = call(
-        pair_kernel, "emb_pair", [block] * ys, [], [place, keep, other], {0: pltpu.SMEM}
-    )
-    parts = list(parts)
-    for k in range(1, ys):
-        parts[k] = lax.ppermute(parts[k], "y", [(y, y ^ k) for y in range(ys)])
+        lambda *refs: pair_kernel(order, *refs), "emb_pair", [block] * ys, [],
+        [place, keep, other], {0: pltpu.SMEM},
+    )
+    parts = [
+        lax.ppermute(part, "y", [(y, y ^ k) for y in range(ys)]) if k else part
+        for k, part in zip(order, parts)
+    ]
     (grad_emb,) = call(last_kernel, "emb_last", [(block[0][::-1], F32)], [], parts)
     return grad_emb, grad_proto
 

time: 164 us -> 159 us (0.970)
  blocking collectives: 123 us -> 113 us
  waiting for transfers between devices: 3.47 us -> 8.58 us
  starting transfers between devices: 15.8 us -> 18.2 us
    all_to_all x1 -> x0, blocking collectives: 10.3 us -> none  [scatter_sum(): return jnp.sum(lax.all_to_all(blocks, axis, 0, 0, tiled=True), axis=0)]
    all_to_all x1, starting transfers between devices: 3.5 us -> 6.44 us  [scatter_sum(): return jnp.sum(lax.all_to_all(blocks, axis, 0, 0, tiled=True), axis=0)]
    ppermute x3, waiting for transfers between devices: 1.92 us -> 4.08 us  [on_device(): lax.ppermute(part, 'y', [(y, y ^ k) for y in range(ys)])]
    ppermute x1, waiting for transfers between devices: 0.01 us -> 1.88 us  [on_device(): other = lax.ppermute(send, 'core', [(0, 1), (1, 0)])]
    pallas_call x12 -> x11, Pallas kernels: 17.1 us -> 17.1 us  [call(): pl.pallas_call(kernel, name=name, out_shape=[dict(out_places)[k](shape, d...]
  transfers between devices with their start and end apart: 5 -> 5, of which waited for: 2 -> 4; matrix products, arithmetic and copies ran while one was open for 1% -> 0% of each run, Pallas kernels for 0% -> 1%
where the time goes in v4:
time: 159 us
  blocking collectives  113 us (71%)
  starting transfers between devices  18.2 us (11%)
  Pallas kernels  17.1 us (11%)
  waiting for transfers between devices  8.58 us (5%)
    all_to_all x8, blocking collectives, to_all(): return lax.all_to_all(copies, axis, 0, 0, tiled=True)  113 us
    pallas_call x11, Pallas kernels, call(): pl.pallas_call(kernel, name=name, out_shape=[dict(out_places)[k](shape, d...  17.1 us
    ppermute x3, starting transfers between devices, on_device(): lax.ppermute(part, 'y', [(y, y ^ k) for y in range(ys)])  9.82 us
    all_to_all x1, starting transfers between devices, scatter_sum(): return jnp.sum(lax.all_to_all(blocks, axis, 0, 0, tiled=True), axis=0)  6.44 us
    ppermute x3, waiting for transfers between devices, on_device(): lax.ppermute(part, 'y', [(y, y ^ k) for y in range(ys)])  4.08 us
  transfers between devices with their start and end apart: 5, of which 4 were waited for; matrix products, arithmetic and copies ran while one was open for 0% of the time, Pallas kernels for 1%

profile of v4, /device:TPU:6, one launch (start us, length us, event | category | flops | bytes accessed | tf_op | source)
XLA Modules:
  0.0 158.5 jit_solution(1615409050168507264)
XLA Ops:
  0.6 0.1 pad_add_fusion.place.refs_0_
  0.7 4.2 %scores.1 = (f32[512,2048]{1,0:T(8,128)S(1)}, bf16[512,2048]{1,0:T(8,128)(2,1)S(1)}, f32[1,2048]{1,0:T(1,128)S(1)}) custom-call(f32[2048,128]{1,0:T(8,128)} %emb.3, f32[512,128]{1,0:T(8,128)} %proto.3, bf16[2048,512]{1,0:T(8,128)(2,1)} %grads.2), custom_call_target="tpu_custom_call" | custom-call | tf_op jit(solution)/shard_map/scores/pallas_call | solution.py:338
  5.0 9.9 %all_to_all.45.parts = f32[8,1,2048]{2,1,0:T(1,128)S(1)} all-to-all(f32[8,1,2048]{2,1,0:T(1,128)S(1)} %broadcast_in_dim.29), channel_id=1, replica_groups=mesh['y'=4,'core'=2,'z'=16,'x'=4] {'y','core'}, dimensions={0} | all-to-all | bytes 131072 | tf_op jit(solution)/shard_map/all_to_all | solution.py:25
  14.9 1.3 col_lse.1
  16.2 0.1 broadcast_in_dim.31
  16.3 34.0 %all_to_all.46.refs_1_ = f32[64,1,512]{2,1,0:T(1,128)S(1)} all-to-all(f32[64,1,512]{2,1,0:T(1,128)S(1)} %broadcast_in_dim.31), channel_id=1, replica_groups=mesh['y'=4,'core'=2,'z'=16,'x'=4] {'z','x'}, dimensions={0} | all-to-all | bytes 262144 | tf_op jit(solution)/shard_map/all_to_all | solution.py:25
  50.3 1.1 row_lse.1
  51.4 8.0 %all_to_all.47.parts = f32[8,1,2048]{2,1,0:T(1,128)S(1)} all-to-all(f32[8,1,2048]{2,1,0:T(1,128)S(1)} %broadcast_in_dim.65), channel_id=1, replica_groups=mesh['y'=4,'core'=2,'z'=16,'x'=4] {'y','core'}, dimensions={0} | all-to-all | bytes 131072 | tf_op jit(solution)/shard_map/all_to_all | solution.py:25
  59.4 1.7 %col_lse_mean.1 = (f32[1,2048]{1,0:T(1,128)S(1)}, f32[2,512]{1,0:T(2,128)S(1)}) custom-call(f32[512,2048]{1,0:T(8,128)S(1)} %get-tuple-element.28.logits.refs_0_, f32[8,1,2048]{2,1,0:T(1,128)S(1)} %all_to_all.47.parts, bf16[512,2048]{1,0:T(8,128)(2,1)S(1)} %get-tuple-element.34.grads.refs_3_), custom_call_target="tpu_custom_call" | custom-call | tf_op jit(solution)/shard_map/col_lse_mean/pallas_call | solution.py:338
  61.1 8.0 %all_to_all.48.parts = f32[4,2,512]{2,1,0:T(2,128)S(1)} all-to-all(f32[4,2,512]{2,1,0:T(2,128)S(1)} %broadcast_in_dim.66), channel_id=1, replica_groups=mesh['y'=4,'core'=2,'z'=16,'x'=4] {'x'}, dimensions={0} | all-to-all | bytes 32768 | tf_op jit(solution)/shard_map/all_to_all | solution.py:25
  69.2 15.4 %all_to_all.49.refs_2_ = f32[16,2,512]{2,1,0:T(2,128)S(1)} all-to-all(f32[16,2,512]{2,1,0:T(2,128)S(1)} %broadcast_in_dim.67), channel_id=1, replica_groups=mesh['y'=4,'core'=2,'z'=16,'x'=4] {'z'}, dimensions={0} | all-to-all | bytes 131072 | tf_op jit(solution)/shard_map/all_to_all | solution.py:25
  84.6 1.2 df2.1
  85.9 8.0 %all_to_all.50.parts = f32[8,1,2048]{2,1,0:T(1,128)S(1)} all-to-all(f32[8,1,2048]{2,1,0:T(1,128)S(1)} %broadcast_in_dim.69), channel_id=1, replica_groups=mesh['y'=4,'core'=2,'z'=16,'x'=4] {'y','core'}, dimensions={0} | all-to-all | bytes 131072 | tf_op jit(solution)/shard_map/all_to_all | solution.py:25
  93.9 1.4 dg1.1
  95.3 0.1 broadcast_in_dim.71
  95.4 21.4 %all_to_all.51.refs_3_ = f32[64,1,512]{2,1,0:T(1,128)S(1)} all-to-all(f32[64,1,512]{2,1,0:T(1,128)S(1)} %broadcast_in_dim.71), channel_id=1, replica_groups=mesh['y'=4,'core'=2,'z'=16,'x'=4] {'z','x'}, dimensions={0} | all-to-all | bytes 262144 | tf_op jit(solution)/shard_map/all_to_all | solution.py:25
  116.8 0.0 copy-start
  116.8 0.0 copy-start.1
  116.8 1.1 df1.1
  118.0 8.0 %all_to_all.52.parts = f32[8,1,2048]{2,1,0:T(1,128)S(1)} all-to-all(f32[8,1,2048]{2,1,0:T(1,128)S(1)} %broadcast_in_dim.73), channel_id=1, replica_groups=mesh['y'=4,'core'=2,'z'=16,'x'=4] {'y','core'}, dimensions={0} | all-to-all | bytes 131072 | tf_op jit(solution)/shard_map/all_to_all | solution.py:25
  126.0 0.0 copy-done
  126.0 0.0 copy-done.1
  126.0 3.6 %grads.3 = (f32[4,128,256]{2,1,0:T(8,128)S(1)}, f32[4,128,256]{2,1,0:T(8,128)S(1)}, f32[512,128]{1,0:T(8,128)}) custom-call(s32[2]{0:T(128)S(1)} %pad_add_fusion.place.refs_0_, f32[512,2048]{1,0:T(8,128)S(1)} %get-tuple-element.28.logits.refs_0_, f32[1,2048]{1,0:T(1,128)S(1)} %get-tuple-element.30.refs_1_.f1, f32[8,1,2048]{2,1,0:T(1,128)S(1)} %all_to_all.52.parts, ...), custom_call_target="tpu_custom_call" | custom-call | tf_op jit(solution)/shard_map/grads/pallas_call | solution.py:338
  129.7 6.4 %all-to-all-start.8 = ((f32[64,8,128]{2,1,0:T(8,128)}), f32[64,8,128]{2,1,0:T(8,128)S(1)}, u32[]{:S(2)}, u32[]{:S(2)}) async-start(f32[64,8,128]{2,1,0:T(8,128)} %bitcast.8), calls=%async_computation.8 | async-start | bytes 524288 | tf_op jit(solution)/shard_map/all_to_all | solution.py:29
  136.1 1.9 %collective-permute-start = (f32[4,128,256]{2,1,0:T(8,128)S(1)}, f32[4,128,256]{2,1,0:T(8,128)S(1)}, u32[]{:S(2)}, u32[]{:S(2)}) collective-permute-start(f32[4,128,256]{2,1,0:T(8,128)S(1)} %get-tuple-element.44), channel_id=1, source_target_pairs={{0,64},{64,0},{1,65},{65,1},{2,66},{66,2},{3,67},{67,3},{4,68},{68... | collective-permute-start | bytes 1572872 | tf_op jit(solution)/shard_map/ppermute | solution.py:414
  138.0 1.9 %collective-permute-done.refs_2_ = f32[4,128,256]{2,1,0:T(8,128)S(1)} collective-permute-done((f32[4,128,256]{2,1,0:T(8,128)S(1)}, f32[4,128,256]{2,1,0:T(8,128)S(1)}, u32[]{:S(2)}, u32[]{:S(2)}) %collective-permute-start) | collective-permute-done | bytes 524320 | tf_op jit(solution)/shard_map/ppermute | solution.py:414
  139.9 0.6 emb_pair.1
  140.5 2.9 %collective-permute-start.1 = (f32[128,256]{1,0:T(8,128)S(1)}, f32[128,256]{1,0:T(8,128)S(1)}, u32[]{:S(2)}, u32[]{:S(2)}) collective-permute-start(f32[128,256]{1,0:T(8,128)S(1)} %get-tuple-element.45), channel_id=1, source_target_pairs={{0,256},{128,384},{256,0},{384,128},{1,257},{129,385},{257,1},{385... | collective-permute-start | bytes 393224 | tf_op jit(solution)/shard_map/ppermute | solution.py:422
  143.5 2.9 %collective-permute-start.2 = (f32[128,256]{1,0:T(8,128)S(1)}, f32[128,256]{1,0:T(8,128)S(1)}, u32[]{:S(2)}, u32[]{:S(2)}) collective-permute-start(f32[128,256]{1,0:T(8,128)S(1)} %get-tuple-element.46), channel_id=1, source_target_pairs={{0,128},{128,0},{256,384},{384,256},{1,129},{129,1},{257,385},{385... | collective-permute-start | bytes 393224 | tf_op jit(solution)/shard_map/ppermute | solution.py:422
  146.4 4.0 %collective-permute-start.3 = (f32[128,256]{1,0:T(8,128)S(1)}, f32[128,256]{1,0:T(8,128)S(1)}, u32[]{:S(2)}, u32[]{:S(2)}) collective-permute-start(f32[128,256]{1,0:T(8,128)S(1)} %get-tuple-element.47), channel_id=1, source_target_pairs={{0,384},{128,256},{256,128},{384,0},{1,385},{129,257},{257,129},{3... | collective-permute-start | bytes 393224 | tf_op jit(solution)/shard_map/ppermute | solution.py:422
  150.4 0.0 collective-permute-done.1.refs_0_
  150.4 0.4 collective-permute-done.2.refs_1_
  150.8 3.7 %collective-permute-done.3.refs_2_ = f32[128,256]{1,0:T(8,128)S(1)} collective-permute-done((f32[128,256]{1,0:T(8,128)S(1)}, f32[128,256]{1,0:T(8,128)S(1)}, u32[]{:S(2)}, u32[]{:S(2)}) %collective-permute-start.3) | collective-permute-done | bytes 131104 | tf_op jit(solution)/shard_map/ppermute | solution.py:422
  154.5 0.8 emb_last.1
  155.2 2.6 %all-to-all-done.8 = f32[64,8,128]{2,1,0:T(8,128)S(1)} async-done(((f32[64,8,128]{2,1,0:T(8,128)}), f32[64,8,128]{2,1,0:T(8,128)S(1)}, u32[]{:S(2)}, u32[]{:S(2)}) %all-to-all-start.8) | async-done | bytes 262176 | tf_op jit(solution)/shard_map/all_to_all | solution.py:29
  157.9 0.7 reduce_sum.9
  (7 shorter events, 0.2 us)
Async XLA Ops:
  116.8 9.2 %copy-start = (f32[2048,128]{1,0:T(8,128)S(1)}, f32[2048,128]{1,0:T(8,128)}, u32[]{:S(2)}) copy-start(f32[2048,128]{1,0:T(8,128)} %emb.3) | copy-start | bytes 3145732
  116.8 9.2 %copy-start.1 = (f32[512,128]{1,0:T(8,128)S(1)}, f32[512,128]{1,0:T(8,128)}, u32[]{:S(2)}) copy-start(f32[512,128]{1,0:T(8,128)} %proto.3) | copy-start | bytes 786436
  129.7 28.2 %all-to-all-start.8 = ((f32[64,8,128]{2,1,0:T(8,128)}), f32[64,8,128]{2,1,0:T(8,128)S(1)}, u32[]{:S(2)}, u32[]{:S(2)}) async-start(f32[64,8,128]{2,1,0:T(8,128)} %bitcast.8), calls=%async_computation.8 | async-start | bytes 524288 | tf_op jit(solution)/shard_map/all_to_all | solution.py:29
  136.1 3.8 %collective-permute-start = (f32[4,128,256]{2,1,0:T(8,128)S(1)}, f32[4,128,256]{2,1,0:T(8,128)S(1)}, u32[]{:S(2)}, u32[]{:S(2)}) collective-permute-start(f32[4,128,256]{2,1,0:T(8,128)S(1)} %get-tuple-element.44), channel_id=1, source_target_pairs={{0,64},{64,0},{1,65},{65,1},{2,66},{66,2},{3,67},{67,3},{4,68},{68... | collective-permute-start | bytes 1572872 | tf_op jit(solution)/shard_map/ppermute | solution.py:414
  140.5 9.8 %collective-permute-start.1 = (f32[128,256]{1,0:T(8,128)S(1)}, f32[128,256]{1,0:T(8,128)S(1)}, u32[]{:S(2)}, u32[]{:S(2)}) collective-permute-start(f32[128,256]{1,0:T(8,128)S(1)} %get-tuple-element.45), channel_id=1, source_target_pairs={{0,256},{128,384},{256,0},{384,128},{1,257},{129,385},{257,1},{385... | collective-permute-start | bytes 393224 | tf_op jit(solution)/shard_map/ppermute | solution.py:422
  143.5 7.3 %collective-permute-start.2 = (f32[128,256]{1,0:T(8,128)S(1)}, f32[128,256]{1,0:T(8,128)S(1)}, u32[]{:S(2)}, u32[]{:S(2)}) collective-permute-start(f32[128,256]{1,0:T(8,128)S(1)} %get-tuple-element.46), channel_id=1, source_target_pairs={{0,128},{128,0},{256,384},{384,256},{1,129},{129,1},{257,385},{385... | collective-permute-start | bytes 393224 | tf_op jit(solution)/shard_map/ppermute | solution.py:422
  146.4 8.1 %collective-permute-start.3 = (f32[128,256]{1,0:T(8,128)S(1)}, f32[128,256]{1,0:T(8,128)S(1)}, u32[]{:S(2)}, u32[]{:S(2)}) collective-permute-start(f32[128,256]{1,0:T(8,128)S(1)} %get-tuple-element.47), channel_id=1, source_target_pairs={{0,384},{128,256},{256,128},{384,0},{1,385},{129,257},{257,129},{3... | collective-permute-start | bytes 393224 | tf_op jit(solution)/shard_map/ppermute | solution.py:422

commit v5 on v4

--- a/solution.py
+++ b/solution.py
@@ -36,13 +36,6 @@
         out.append(piece)
         x = x - piece.astype(F32)
     return out
-
-
-def times(left, right):
-    hi, low = split(right, 2)
-    both = jnp.dot(jnp.concatenate(left, axis=0), hi, preferred_element_type=F32)
-    size = left[0].shape[0]
-    return both[:size] + both[size:] + jnp.dot(left[0], low, preferred_element_type=F32)
 
 
 def down(row):
@@ -123,6 +116,7 @@
 
 def col_kernel(logits, parts, f1, lse_out, shifts, peaks, masses):
     tiles = logits.shape[1] // LANES
+    count = logits.shape[0] // 8
     f1[...] = -merge_parts(parts)
     shifts[...] = jnp.broadcast_to(f1[...], shifts.shape)
 
@@ -139,7 +133,7 @@
         masses[rows, :] = mass
         return 0
 
-    lax.fori_loop(0, logits.shape[0] // 8, step, 0, unroll=4)
+    lax.fori_loop(0, count, step, 0, unroll=count)
     peak_t = jnp.transpose(peaks[...])
     peak = jnp.max(peak_t, axis=0, keepdims=True)
     mass = jnp.sum(jnp.transpose(masses[...]) * jnp.exp2(peak_t - peak), axis=0, keepdims=True)
@@ -154,6 +148,7 @@
 
 def col_mean_kernel(logits, parts, grads, f2, out, shifts, peaks, masses, means):
     tiles = logits.shape[1] // LANES
+    count = logits.shape[0] // 16
     f2[...] = -merge_parts(parts)
     shifts[...] = jnp.broadcast_to(f2[...], shifts.shape)
 
@@ -173,7 +168,7 @@
         means[rows, :] = mean
         return 0
 
-    lax.fori_loop(0, logits.shape[0] // 16, step, 0, unroll=2)
+    lax.fori_loop(0, count, step, 0, unroll=count)
     peak_t = jnp.transpose(peaks[...])
     peak = jnp.max(peak_t, axis=0, keepdims=True)
     share = jnp.exp2(peak_t - peak)
@@ -245,6 +240,7 @@
 
 def dg1_kernel(logits, f2, g1, parts, score, rest, out, rows_of, weights, cols, sums):
     tiles = logits.shape[1] // LANES
+    count = logits.shape[0] // 8
     rows_of[...] = jnp.broadcast_to(f2[...], rows_of.shape)
     weights[...] = jnp.broadcast_to(add_parts(parts), weights.shape)
     cols[...] = down(g1[...])
@@ -261,17 +257,8 @@
         sums[rows, :] = total
         return 0
 
-    lax.fori_loop(0, logits.shape[0] // 8, step, 0, unroll=4)
+    lax.fori_loop(0, count, step, 0, unroll=count)
     out[...] = -jnp.sum(jnp.transpose(sums[...]), axis=0, keepdims=True)
-
-
-def proto_term(score, emb):
-    width = emb.shape[1]
-    s_hi, s_low = split(score, 2)
-    e_hi, e_low = split(emb * INV_EPS, 2)
-    both = jnp.dot(s_hi, jnp.concatenate([e_hi, e_low], axis=1), preferred_element_type=F32)
-    low = jnp.dot(s_low, e_hi, preferred_element_type=F32)
-    return both[:, :width] + both[:, width:] + low
 
 
 def df1_kernel(log_mass, logits, f1, g1, parts, score, rest, out, cols, weights):
@@ -297,25 +284,38 @@
             out[:, s] = -jnp.sum(t, axis=0, keepdims=True)
 
 
-def grads_kernel(place, logits, f1, parts, score, emb, proto, keep, send, proto_out):
+def grads_kernel(place, logits, f1, parts, score, emb, proto, keep, send, proto_out, total, sem):
     df1 = add_parts(parts)
-    turned_p = split(jnp.transpose(proto[...]) * INV_EPS, 2)
+    width = emb.shape[1]
     size = keep.shape[2]
     step = 4 * size
-    total = jnp.zeros(proto_out.shape, F32)
+    pieces = []
+    sums = jnp.zeros(total.shape, F32)
     for at in range(0, logits.shape[1], step):
         nodes = slice(at, at + step)
         dlog = score[:, nodes] - jnp.exp2(logits[:, nodes] + f1[:, nodes]) * df1[:, nodes]
-        part = times(turned_p, dlog)
+        hi, low = split(dlog, 2)
+        pieces.append((hi, low))
+        e_hi, e_low = split(emb[nodes, :] * INV_EPS, 2)
+        both = jnp.dot(hi, jnp.concatenate([e_hi, e_low], axis=1), preferred_element_type=F32)
+        sums = sums + both[:, :width] + both[:, width:]
+        sums = sums + jnp.dot(low, e_hi, preferred_element_type=F32)
+    total[...] = sums
+    write = pltpu.make_async_copy(total, proto_out, sem)
+    write.start()
+    p_hi, p_low = split(jnp.transpose(proto[...]) * INV_EPS, 2)
+    p_both = jnp.concatenate([p_hi, p_low], axis=0)
+    first = place[1] == 0
+    for at, (hi, low) in enumerate(pieces):
+        both = jnp.dot(p_both, hi, preferred_element_type=F32)
+        part = both[:width] + both[width:] + jnp.dot(p_hi, low, preferred_element_type=F32)
         for k in range(0, step // size, 2):
-            y = (at // size + k) // 2
+            y = (at * (step // size) + k) // 2
             even = part[:, k * size : (k + 1) * size]
             odd = part[:, (k + 1) * size : (k + 2) * size]
-            first = place[1] == 0
             keep[y] = jnp.where(first, even, odd)
             send[y] = jnp.where(first, odd, even)
-        total = total + proto_term(dlog, emb[nodes, :])
-    proto_out[...] = total
+    write.wait()
 
 
 def pair_kernel(order, place, keep, other, *outs):
@@ -388,7 +388,7 @@
     )
     g1, here = call(
         lambda *refs: row_kernel(log_mass, *refs), "row_lse", [col, row], [tall],
-        [logits, to_all(here, node)],
+        [logits, to_all(here, ("x", "z"))],
     )
     f2, here = call(
         col_mean_kernel, "col_lse_mean", [row, two],
@@ -405,11 +405,13 @@
     )
     score, here = call(
         lambda *refs: df1_kernel(log_mass, *refs), "df1", [full, row], [tall, tall],
-        [logits, f1, g1, to_all(here, node), score],
+        [logits, f1, g1, to_all(here, ("x", "z")), score],
     )
     keep, send, proto_part = call(
-        grads_kernel, "grads", [blocks, blocks, ((local, width), F32)], [],
-        [place, logits, f1, to_all(here, comm), score, embeddings, prototypes], {0: pltpu.SMEM},
+        grads_kernel, "grads", [blocks, blocks, ((local, width), F32)],
+        [(local, width), pltpu.SemaphoreType.DMA],
+        [place, logits, f1, to_all(here, comm), score, embeddings, prototypes],
+        {0: pltpu.SMEM}, {2: hbm},
     )
     other = lax.ppermute(send, "core", [(0, 1), (1, 0)])
     grad_proto = scatter_sum(proto_part.reshape(xs * zs, -1, width), node)

time: 159 us -> 157 us (0.987)
  Pallas kernels: 17.1 us -> 15.3 us
    pallas_call x11, Pallas kernels: 17.1 us -> 15.3 us  [call(): pl.pallas_call(kernel, name=name, out_shape=[dict(out_places)[k](shape, d...]
where the time goes in v5:
time: 157 us; the launch traced here: 156 us
  blocking collectives  113 us (72%)
  starting transfers between devices  17.9 us (11%)
  Pallas kernels  15.3 us (10%)
  waiting for transfers between devices  8.23 us (5%)
    all_to_all x8, blocking collectives, to_all(): return lax.all_to_all(copies, axis, 0, 0, tiled=True)  113 us
    pallas_call x11, Pallas kernels, call(): pl.pallas_call(kernel, name=name, out_shape=[dict(out_places)[k](shape, d...  15.3 us
    ppermute x3, starting transfers between devices, on_device(): lax.ppermute(part, 'y', [(y, y ^ k) for y in range(ys)])  9.82 us
    all_to_all x1, starting transfers between devices, scatter_sum(): return jnp.sum(lax.all_to_all(blocks, axis, 0, 0, tiled=True), axis=0)  6.21 us
    ppermute x3, waiting for transfers between devices, on_device(): lax.ppermute(part, 'y', [(y, y ^ k) for y in range(ys)])  4.08 us
  transfers between devices with their start and end apart: 5, of which 4 were waited for; matrix products, arithmetic and copies ran while one was open for 0% of the time, Pallas kernels for 1%

profile of v5, /device:TPU:6, one launch (start us, length us, event | category | flops | bytes accessed | tf_op | source)
XLA Modules:
  0.0 156.0 jit_solution(18274935175534871218)
XLA Ops:
  0.6 0.1 pad_add_fusion.place.refs_0_
  0.7 4.2 %scores.1 = (f32[512,2048]{1,0:T(8,128)S(1)}, bf16[512,2048]{1,0:T(8,128)(2,1)S(1)}, f32[1,2048]{1,0:T(1,128)S(1)}) custom-call(f32[2048,128]{1,0:T(8,128)} %emb.3, f32[512,128]{1,0:T(8,128)} %proto.3, bf16[2048,512]{1,0:T(8,128)(2,1)} %grads.2), custom_call_target="tpu_custom_call" | custom-call | tf_op jit(solution)/shard_map/scores/pallas_call | solution.py:338
  5.0 9.9 %all_to_all.45.parts = f32[8,1,2048]{2,1,0:T(1,128)S(1)} all-to-all(f32[8,1,2048]{2,1,0:T(1,128)S(1)} %broadcast_in_dim.29), channel_id=1, replica_groups=mesh['y'=4,'core'=2,'z'=16,'x'=4] {'y','core'}, dimensions={0} | all-to-all | bytes 131072 | tf_op jit(solution)/shard_map/all_to_all | solution.py:25
  14.9 1.0 col_lse.1
  15.9 0.1 broadcast_in_dim.31
  15.9 34.0 %all_to_all.46.refs_1_ = f32[64,1,512]{2,1,0:T(1,128)S(1)} all-to-all(f32[64,1,512]{2,1,0:T(1,128)S(1)} %broadcast_in_dim.31), channel_id=1, replica_groups=mesh['y'=4,'core'=2,'z'=16,'x'=4] {'x','z'}, dimensions={0} | all-to-all | bytes 262144 | tf_op jit(solution)/shard_map/all_to_all | solution.py:25
  49.9 1.0 row_lse.1
  51.0 8.0 %all_to_all.47.parts = f32[8,1,2048]{2,1,0:T(1,128)S(1)} all-to-all(f32[8,1,2048]{2,1,0:T(1,128)S(1)} %broadcast_in_dim.65), channel_id=1, replica_groups=mesh['y'=4,'core'=2,'z'=16,'x'=4] {'y','core'}, dimensions={0} | all-to-all | bytes 131072 | tf_op jit(solution)/shard_map/all_to_all | solution.py:25
  59.0 1.5 col_lse_mean.1
  60.5 7.8 %all_to_all.48.parts = f32[4,2,512]{2,1,0:T(2,128)S(1)} all-to-all(f32[4,2,512]{2,1,0:T(2,128)S(1)} %broadcast_in_dim.66), channel_id=1, replica_groups=mesh['y'=4,'core'=2,'z'=16,'x'=4] {'x'}, dimensions={0} | all-to-all | bytes 32768 | tf_op jit(solution)/shard_map/all_to_all | solution.py:25
  68.3 15.5 %all_to_all.49.refs_2_ = f32[16,2,512]{2,1,0:T(2,128)S(1)} all-to-all(f32[16,2,512]{2,1,0:T(2,128)S(1)} %broadcast_in_dim.67), channel_id=1, replica_groups=mesh['y'=4,'core'=2,'z'=16,'x'=4] {'z'}, dimensions={0} | all-to-all | bytes 131072 | tf_op jit(solution)/shard_map/all_to_all | solution.py:25
  83.9 1.2 df2.1
  85.1 8.0 %all_to_all.50.parts = f32[8,1,2048]{2,1,0:T(1,128)S(1)} all-to-all(f32[8,1,2048]{2,1,0:T(1,128)S(1)} %broadcast_in_dim.69), channel_id=1, replica_groups=mesh['y'=4,'core'=2,'z'=16,'x'=4] {'y','core'}, dimensions={0} | all-to-all | bytes 131072 | tf_op jit(solution)/shard_map/all_to_all | solution.py:25
  93.1 1.0 dg1.1
  94.2 0.1 broadcast_in_dim.71
  94.3 21.4 %all_to_all.51.refs_3_ = f32[64,1,512]{2,1,0:T(1,128)S(1)} all-to-all(f32[64,1,512]{2,1,0:T(1,128)S(1)} %broadcast_in_dim.71), channel_id=1, replica_groups=mesh['y'=4,'core'=2,'z'=16,'x'=4] {'x','z'}, dimensions={0} | all-to-all | bytes 262144 | tf_op jit(solution)/shard_map/all_to_all | solution.py:25
  115.7 0.0 copy-start
  115.7 0.0 copy-start.1
  115.7 1.2 df1.1
  116.9 8.0 %all_to_all.52.parts = f32[8,1,2048]{2,1,0:T(1,128)S(1)} all-to-all(f32[8,1,2048]{2,1,0:T(1,128)S(1)} %broadcast_in_dim.73), channel_id=1, replica_groups=mesh['y'=4,'core'=2,'z'=16,'x'=4] {'y','core'}, dimensions={0} | all-to-all | bytes 131072 | tf_op jit(solution)/shard_map/all_to_all | solution.py:25
  124.9 0.0 copy-done
  124.9 0.0 copy-done.1
  124.9 2.8 %grads.3 = (f32[4,128,256]{2,1,0:T(8,128)S(1)}, f32[4,128,256]{2,1,0:T(8,128)S(1)}, f32[512,128]{1,0:T(8,128)}) custom-call(s32[2]{0:T(128)S(1)} %pad_add_fusion.place.refs_0_, f32[512,2048]{1,0:T(8,128)S(1)} %get-tuple-element.28.logits.refs_0_, f32[1,2048]{1,0:T(1,128)S(1)} %get-tuple-element.30.refs_1_.f1, f32[8,1,2048]{2,1,0:T(1,128)S(1)} %all_to_all.52.parts, ...), custom_call_target="tpu_custom_call" | custom-call | tf_op jit(solution)/shard_map/grads/pallas_call | solution.py:338
  127.7 6.2 %all-to-all-start.8 = ((f32[64,8,128]{2,1,0:T(8,128)}), f32[64,8,128]{2,1,0:T(8,128)S(1)}, u32[]{:S(2)}, u32[]{:S(2)}) async-start(f32[64,8,128]{2,1,0:T(8,128)} %bitcast.15), calls=%async_computation.8 | async-start | bytes 524288 | tf_op jit(solution)/shard_map/all_to_all | solution.py:29
  133.9 1.9 %collective-permute-start = (f32[4,128,256]{2,1,0:T(8,128)S(1)}, f32[4,128,256]{2,1,0:T(8,128)S(1)}, u32[]{:S(2)}, u32[]{:S(2)}) collective-permute-start(f32[4,128,256]{2,1,0:T(8,128)S(1)} %get-tuple-element.44), channel_id=1, source_target_pairs={{0,64},{64,0},{1,65},{65,1},{2,66},{66,2},{3,67},{67,3},{4,68},{68... | collective-permute-start | bytes 1572872 | tf_op jit(solution)/shard_map/ppermute | solution.py:416
  135.8 1.9 %collective-permute-done.refs_2_ = f32[4,128,256]{2,1,0:T(8,128)S(1)} collective-permute-done((f32[4,128,256]{2,1,0:T(8,128)S(1)}, f32[4,128,256]{2,1,0:T(8,128)S(1)}, u32[]{:S(2)}, u32[]{:S(2)}) %collective-permute-start) | collective-permute-done | bytes 524320 | tf_op jit(solution)/shard_map/ppermute | solution.py:416
  137.7 0.6 emb_pair.1
  138.3 2.9 %collective-permute-start.1 = (f32[128,256]{1,0:T(8,128)S(1)}, f32[128,256]{1,0:T(8,128)S(1)}, u32[]{:S(2)}, u32[]{:S(2)}) collective-permute-start(f32[128,256]{1,0:T(8,128)S(1)} %get-tuple-element.45), channel_id=1, source_target_pairs={{0,256},{128,384},{256,0},{384,128},{1,257},{129,385},{257,1},{385... | collective-permute-start | bytes 393224 | tf_op jit(solution)/shard_map/ppermute | solution.py:424
  141.2 2.9 %collective-permute-start.2 = (f32[128,256]{1,0:T(8,128)S(1)}, f32[128,256]{1,0:T(8,128)S(1)}, u32[]{:S(2)}, u32[]{:S(2)}) collective-permute-start(f32[128,256]{1,0:T(8,128)S(1)} %get-tuple-element.46), channel_id=1, source_target_pairs={{0,128},{128,0},{256,384},{384,256},{1,129},{129,1},{257,385},{385... | collective-permute-start | bytes 393224 | tf_op jit(solution)/shard_map/ppermute | solution.py:424
  144.2 4.0 %collective-permute-start.3 = (f32[128,256]{1,0:T(8,128)S(1)}, f32[128,256]{1,0:T(8,128)S(1)}, u32[]{:S(2)}, u32[]{:S(2)}) collective-permute-start(f32[128,256]{1,0:T(8,128)S(1)} %get-tuple-element.47), channel_id=1, source_target_pairs={{0,384},{128,256},{256,128},{384,0},{1,385},{129,257},{257,129},{3... | collective-permute-start | bytes 393224 | tf_op jit(solution)/shard_map/ppermute | solution.py:424
  148.2 0.0 collective-permute-done.1.refs_0_
  148.2 0.4 collective-permute-done.2.refs_1_
  148.6 3.7 %collective-permute-done.3.refs_2_ = f32[128,256]{1,0:T(8,128)S(1)} collective-permute-done((f32[128,256]{1,0:T(8,128)S(1)}, f32[128,256]{1,0:T(8,128)S(1)}, u32[]{:S(2)}, u32[]{:S(2)}) %collective-permute-start.3) | collective-permute-done | bytes 131104 | tf_op jit(solution)/shard_map/ppermute | solution.py:424
  152.3 0.8 emb_last.1
  153.0 2.3 %all-to-all-done.8 = f32[64,8,128]{2,1,0:T(8,128)S(1)} async-done(((f32[64,8,128]{2,1,0:T(8,128)}), f32[64,8,128]{2,1,0:T(8,128)S(1)}, u32[]{:S(2)}, u32[]{:S(2)}) %all-to-all-start.8) | async-done | bytes 262176 | tf_op jit(solution)/shard_map/all_to_all | solution.py:29
  155.3 0.7 reduce_sum.9
  (7 shorter events, 0.2 us)
Async XLA Ops:
  115.7 9.2 %copy-start = (f32[2048,128]{1,0:T(8,128)S(1)}, f32[2048,128]{1,0:T(8,128)}, u32[]{:S(2)}) copy-start(f32[2048,128]{1,0:T(8,128)} %emb.3) | copy-start | bytes 3145732
  115.7 9.2 %copy-start.1 = (f32[512,128]{1,0:T(8,128)S(1)}, f32[512,128]{1,0:T(8,128)}, u32[]{:S(2)}) copy-start(f32[512,128]{1,0:T(8,128)} %proto.3) | copy-start | bytes 786436
  127.7 27.6 %all-to-all-start.8 = ((f32[64,8,128]{2,1,0:T(8,128)}), f32[64,8,128]{2,1,0:T(8,128)S(1)}, u32[]{:S(2)}, u32[]{:S(2)}) async-start(f32[64,8,128]{2,1,0:T(8,128)} %bitcast.15), calls=%async_computation.8 | async-start | bytes 524288 | tf_op jit(solution)/shard_map/all_to_all | solution.py:29
  133.9 3.8 %collective-permute-start = (f32[4,128,256]{2,1,0:T(8,128)S(1)}, f32[4,128,256]{2,1,0:T(8,128)S(1)}, u32[]{:S(2)}, u32[]{:S(2)}) collective-permute-start(f32[4,128,256]{2,1,0:T(8,128)S(1)} %get-tuple-element.44), channel_id=1, source_target_pairs={{0,64},{64,0},{1,65},{65,1},{2,66},{66,2},{3,67},{67,3},{4,68},{68... | collective-permute-start | bytes 1572872 | tf_op jit(solution)/shard_map/ppermute | solution.py:416
  138.3 9.8 %collective-permute-start.1 = (f32[128,256]{1,0:T(8,128)S(1)}, f32[128,256]{1,0:T(8,128)S(1)}, u32[]{:S(2)}, u32[]{:S(2)}) collective-permute-start(f32[128,256]{1,0:T(8,128)S(1)} %get-tuple-element.45), channel_id=1, source_target_pairs={{0,256},{128,384},{256,0},{384,128},{1,257},{129,385},{257,1},{385... | collective-permute-start | bytes 393224 | tf_op jit(solution)/shard_map/ppermute | solution.py:424
  141.2 7.3 %collective-permute-start.2 = (f32[128,256]{1,0:T(8,128)S(1)}, f32[128,256]{1,0:T(8,128)S(1)}, u32[]{:S(2)}, u32[]{:S(2)}) collective-permute-start(f32[128,256]{1,0:T(8,128)S(1)} %get-tuple-element.46), channel_id=1, source_target_pairs={{0,128},{128,0},{256,384},{384,256},{1,129},{129,1},{257,385},{385... | collective-permute-start | bytes 393224 | tf_op jit(solution)/shard_map/ppermute | solution.py:424
  144.2 8.1 %collective-permute-start.3 = (f32[128,256]{1,0:T(8,128)S(1)}, f32[128,256]{1,0:T(8,128)S(1)}, u32[]{:S(2)}, u32[]{:S(2)}) collective-permute-start(f32[128,256]{1,0:T(8,128)S(1)} %get-tuple-element.47), channel_id=1, source_target_pairs={{0,384},{128,256},{256,128},{384,0},{1,385},{129,257},{257,129},{3... | collective-permute-start | bytes 393224 | tf_op jit(solution)/shard_map/ppermute | solution.py:424

commit v6 on v5

--- a/solution.py
+++ b/solution.py
@@ -23,10 +23,6 @@
     count = lax.axis_size(axis)
     copies = jnp.broadcast_to(values[None], (count,) + values.shape)
     return lax.all_to_all(copies, axis, 0, 0, tiled=True)
-
-
-def scatter_sum(blocks, axis):
-    return jnp.sum(lax.all_to_all(blocks, axis, 0, 0, tiled=True), axis=0)
 
 
 def split(x, pieces):
@@ -290,7 +286,7 @@
     size = keep.shape[2]
     step = 4 * size
     pieces = []
-    sums = jnp.zeros(total.shape, F32)
+    sums = jnp.zeros((logits.shape[0], width), F32)
     for at in range(0, logits.shape[1], step):
         nodes = slice(at, at + step)
         dlog = score[:, nodes] - jnp.exp2(logits[:, nodes] + f1[:, nodes]) * df1[:, nodes]
@@ -300,7 +296,11 @@
         both = jnp.dot(hi, jnp.concatenate([e_hi, e_low], axis=1), preferred_element_type=F32)
         sums = sums + both[:, :width] + both[:, width:]
         sums = sums + jnp.dot(low, e_hi, preferred_element_type=F32)
-    total[...] = sums
+    xs, zs, tall, _ = total.shape
+    for x in range(xs):
+        for z in range(zs):
+            start = (z * xs + x) * tall
+            total[x, z] = sums[start : start + tall]
     write = pltpu.make_async_copy(total, proto_out, sem)
     write.start()
     p_hi, p_low = split(jnp.transpose(proto[...]) * INV_EPS, 2)
@@ -324,12 +324,9 @@
         out[...] = keep[y] + other[y]
 
 
-def last_kernel(*refs):
-    *parts, out = refs
-    total = parts[0][...]
-    for part in parts[1:]:
-        total = total + part[...]
-    out[...] = jnp.transpose(total)
+def last_kernel(far, near, next_to, own, blocks, emb_out, proto_out):
+    emb_out[...] = jnp.transpose((far[...] + near[...]) + (next_to[...] + own[...]))
+    proto_out[...] = add_parts(blocks)
 
 
 def call(kernel, name, outs, scratch, args, in_places=(), out_places=()):
@@ -371,6 +368,7 @@
     blocks = ((ys,) + block[0], F32)
     node = ("z", "x")
     comm = ("y", "core")
+    by_node = ((xs, zs, local // (xs * zs), width), F32)
     hbm = pltpu.HBM
     place = jnp.stack([lax.axis_index("y"), lax.axis_index("core")])
 
@@ -408,13 +406,14 @@
         [logits, f1, g1, to_all(here, ("x", "z")), score],
     )
     keep, send, proto_part = call(
-        grads_kernel, "grads", [blocks, blocks, ((local, width), F32)],
-        [(local, width), pltpu.SemaphoreType.DMA],
+        grads_kernel, "grads", [blocks, blocks, by_node],
+        [by_node[0], pltpu.SemaphoreType.DMA],
         [place, logits, f1, to_all(here, comm), score, embeddings, prototypes],
         {0: pltpu.SMEM}, {2: hbm},
     )
     other = lax.ppermute(send, "core", [(0, 1), (1, 0)])
-    grad_proto = scatter_sum(proto_part.reshape(xs * zs, -1, width), node)
+    proto_part = proto_part.reshape(xs * zs, -1, width)
+    proto_part = lax.all_to_all(proto_part, ("x", "z"), 0, 0, tiled=True)
     order = (2, 1, 3, 0)
     parts = call(
         lambda *refs: pair_kernel(order, *refs), "emb_pair", [block] * ys, [],
@@ -424,7 +423,10 @@
         lax.ppermute(part, "y", [(y, y ^ k) for y in range(ys)]) if k else part
         for k, part in zip(order, parts)
     ]
-    (grad_emb,) = call(last_kernel, "emb_last", [(block[0][::-1], F32)], [], parts)
+    grad_emb, grad_proto = call(
+        last_kernel, "last", [(block[0][::-1], F32), (proto_part.shape[1:], F32)], [],
+        parts + [proto_part],
+    )
     return grad_emb, grad_proto
 
 

time: 157 us -> 156 us (level)
  transfers between devices with their start and end apart: 5 -> 5, of which waited for: 4 -> 4; matrix products, arithmetic and copies ran while one was open for 0% -> 0% of each run, Pallas kernels for 1% -> 0%
where the time goes in v6:
time: 156 us
  blocking collectives  113 us (72%)
  starting transfers between devices  18.1 us (12%)
  Pallas kernels  15.2 us (10%)
  waiting for transfers between devices  8.36 us (5%)
    all_to_all x8, blocking collectives, to_all(): return lax.all_to_all(copies, axis, 0, 0, tiled=True)  113 us
    pallas_call x11, Pallas kernels, call(): pl.pallas_call(kernel, name=name, out_shape=[dict(out_places)[k](shape, d...  15.2 us
    ppermute x3, starting transfers between devices, on_device(): lax.ppermute(part, 'y', [(y, y ^ k) for y in range(ys)])  9.82 us
    all_to_all x1, starting transfers between devices, on_device(): proto_part = lax.all_to_all(proto_part, ('x', 'z'), 0, 0, tiled=True)  6.41 us
    ppermute x3, waiting for transfers between devices, on_device(): lax.ppermute(part, 'y', [(y, y ^ k) for y in range(ys)])  4.08 us
  transfers between devices with their start and end apart: 5, of which 4 were waited for; matrix products, arithmetic and copies ran while one was open for 0% of the time, Pallas kernels for 0%

profile of v6, /device:TPU:6, one launch (start us, length us, event | category | flops | bytes accessed | tf_op | source)
XLA Modules:
  0.0 155.5 jit_solution(16791586201161954574)
XLA Ops:
  0.6 0.1 pad_add_fusion.place.refs_0_
  0.7 4.2 %scores.1 = (f32[512,2048]{1,0:T(8,128)S(1)}, bf16[512,2048]{1,0:T(8,128)(2,1)S(1)}, f32[1,2048]{1,0:T(1,128)S(1)}) custom-call(f32[2048,128]{1,0:T(8,128)} %emb.3, f32[512,128]{1,0:T(8,128)} %proto.3, bf16[2048,512]{1,0:T(8,128)(2,1)} %grads.2), custom_call_target="tpu_custom_call" | custom-call | tf_op jit(solution)/shard_map/scores/pallas_call | solution.py:335
  5.0 9.9 %all_to_all.45.parts = f32[8,1,2048]{2,1,0:T(1,128)S(1)} all-to-all(f32[8,1,2048]{2,1,0:T(1,128)S(1)} %broadcast_in_dim.29), channel_id=1, replica_groups=mesh['y'=4,'core'=2,'z'=16,'x'=4] {'y','core'}, dimensions={0} | all-to-all | bytes 131072 | tf_op jit(solution)/shard_map/all_to_all | solution.py:25
  14.9 1.0 col_lse.1
  15.9 0.1 broadcast_in_dim.31
  16.0 34.0 %all_to_all.46.refs_1_ = f32[64,1,512]{2,1,0:T(1,128)S(1)} all-to-all(f32[64,1,512]{2,1,0:T(1,128)S(1)} %broadcast_in_dim.31), channel_id=1, replica_groups=mesh['y'=4,'core'=2,'z'=16,'x'=4] {'x','z'}, dimensions={0} | all-to-all | bytes 262144 | tf_op jit(solution)/shard_map/all_to_all | solution.py:25
  49.9 1.1 row_lse.1
  51.1 8.0 %all_to_all.47.parts = f32[8,1,2048]{2,1,0:T(1,128)S(1)} all-to-all(f32[8,1,2048]{2,1,0:T(1,128)S(1)} %broadcast_in_dim.65), channel_id=1, replica_groups=mesh['y'=4,'core'=2,'z'=16,'x'=4] {'y','core'}, dimensions={0} | all-to-all | bytes 131072 | tf_op jit(solution)/shard_map/all_to_all | solution.py:25
  59.1 1.4 col_lse_mean.1
  60.5 7.8 %all_to_all.48.parts = f32[4,2,512]{2,1,0:T(2,128)S(1)} all-to-all(f32[4,2,512]{2,1,0:T(2,128)S(1)} %broadcast_in_dim.66), channel_id=1, replica_groups=mesh['y'=4,'core'=2,'z'=16,'x'=4] {'x'}, dimensions={0} | all-to-all | bytes 32768 | tf_op jit(solution)/shard_map/all_to_all | solution.py:25
  68.3 15.5 %all_to_all.49.refs_2_ = f32[16,2,512]{2,1,0:T(2,128)S(1)} all-to-all(f32[16,2,512]{2,1,0:T(2,128)S(1)} %broadcast_in_dim.67), channel_id=1, replica_groups=mesh['y'=4,'core'=2,'z'=16,'x'=4] {'z'}, dimensions={0} | all-to-all | bytes 131072 | tf_op jit(solution)/shard_map/all_to_all | solution.py:25
  83.8 1.2 df2.1
  85.1 8.0 %all_to_all.50.parts = f32[8,1,2048]{2,1,0:T(1,128)S(1)} all-to-all(f32[8,1,2048]{2,1,0:T(1,128)S(1)} %broadcast_in_dim.69), channel_id=1, replica_groups=mesh['y'=4,'core'=2,'z'=16,'x'=4] {'y','core'}, dimensions={0} | all-to-all | bytes 131072 | tf_op jit(solution)/shard_map/all_to_all | solution.py:25
  93.1 1.0 dg1.1
  94.1 0.1 broadcast_in_dim.71
  94.2 21.4 %all_to_all.51.refs_3_ = f32[64,1,512]{2,1,0:T(1,128)S(1)} all-to-all(f32[64,1,512]{2,1,0:T(1,128)S(1)} %broadcast_in_dim.71), channel_id=1, replica_groups=mesh['y'=4,'core'=2,'z'=16,'x'=4] {'x','z'}, dimensions={0} | all-to-all | bytes 262144 | tf_op jit(solution)/shard_map/all_to_all | solution.py:25
  115.6 0.0 copy-start
  115.6 0.0 copy-start.1
  115.6 1.1 df1.1
  116.8 8.0 %all_to_all.52.parts = f32[8,1,2048]{2,1,0:T(1,128)S(1)} all-to-all(f32[8,1,2048]{2,1,0:T(1,128)S(1)} %broadcast_in_dim.73), channel_id=1, replica_groups=mesh['y'=4,'core'=2,'z'=16,'x'=4] {'y','core'}, dimensions={0} | all-to-all | bytes 131072 | tf_op jit(solution)/shard_map/all_to_all | solution.py:25
  124.8 0.0 copy-done
  124.8 0.0 copy-done.1
  124.8 2.8 %grads.3 = (f32[4,128,256]{2,1,0:T(8,128)S(1)}, f32[4,128,256]{2,1,0:T(8,128)S(1)}, f32[4,16,8,128]{3,2,1,0:T(8,128)}) custom-call(s32[2]{0:T(128)S(1)} %pad_add_fusion.place.refs_0_, f32[512,2048]{1,0:T(8,128)S(1)} %get-tuple-element.28.logits.refs_0_, f32[1,2048]{1,0:T(1,128)S(1)} %get-tuple-element.30.refs_1_.f1, f32[8,1,2048]{2,1,0:T(1,128)S(1)} %all_to_all.52.parts, ...), custom_call_target="tpu_custom_call" | custom-call | tf_op jit(solution)/shard_map/grads/pallas_call | solution.py:335
  127.6 6.4 %all-to-all-start.8 = ((f32[64,8,128]{2,1,0:T(8,128)}), f32[64,8,128]{2,1,0:T(8,128)S(1)}, u32[]{:S(2)}, u32[]{:S(2)}) async-start(f32[64,8,128]{2,1,0:T(8,128)} %bitcast.15), calls=%async_computation.8 | async-start | bytes 524288 | tf_op jit(solution)/shard_map/all_to_all | solution.py:416
  134.0 1.9 %collective-permute-start = (f32[4,128,256]{2,1,0:T(8,128)S(1)}, f32[4,128,256]{2,1,0:T(8,128)S(1)}, u32[]{:S(2)}, u32[]{:S(2)}) collective-permute-start(f32[4,128,256]{2,1,0:T(8,128)S(1)} %get-tuple-element.44), channel_id=1, source_target_pairs={{0,64},{64,0},{1,65},{65,1},{2,66},{66,2},{3,67},{67,3},{4,68},{68... | collective-permute-start | bytes 1572872 | tf_op jit(solution)/shard_map/ppermute | solution.py:414
  135.9 1.9 %collective-permute-done.refs_2_ = f32[4,128,256]{2,1,0:T(8,128)S(1)} collective-permute-done((f32[4,128,256]{2,1,0:T(8,128)S(1)}, f32[4,128,256]{2,1,0:T(8,128)S(1)}, u32[]{:S(2)}, u32[]{:S(2)}) %collective-permute-start) | collective-permute-done | bytes 524320 | tf_op jit(solution)/shard_map/ppermute | solution.py:414
  137.8 0.6 emb_pair.1
  138.4 2.9 %collective-permute-start.1 = (f32[128,256]{1,0:T(8,128)S(1)}, f32[128,256]{1,0:T(8,128)S(1)}, u32[]{:S(2)}, u32[]{:S(2)}) collective-permute-start(f32[128,256]{1,0:T(8,128)S(1)} %get-tuple-element.45), channel_id=1, source_target_pairs={{0,256},{128,384},{256,0},{384,128},{1,257},{129,385},{257,1},{385... | collective-permute-start | bytes 393224 | tf_op jit(solution)/shard_map/ppermute | solution.py:423
  141.3 2.9 %collective-permute-start.2 = (f32[128,256]{1,0:T(8,128)S(1)}, f32[128,256]{1,0:T(8,128)S(1)}, u32[]{:S(2)}, u32[]{:S(2)}) collective-permute-start(f32[128,256]{1,0:T(8,128)S(1)} %get-tuple-element.46), channel_id=1, source_target_pairs={{0,128},{128,0},{256,384},{384,256},{1,129},{129,1},{257,385},{385... | collective-permute-start | bytes 393224 | tf_op jit(solution)/shard_map/ppermute | solution.py:423
  144.3 4.0 %collective-permute-start.3 = (f32[128,256]{1,0:T(8,128)S(1)}, f32[128,256]{1,0:T(8,128)S(1)}, u32[]{:S(2)}, u32[]{:S(2)}) collective-permute-start(f32[128,256]{1,0:T(8,128)S(1)} %get-tuple-element.47), channel_id=1, source_target_pairs={{0,384},{128,256},{256,128},{384,0},{1,385},{129,257},{257,129},{3... | collective-permute-start | bytes 393224 | tf_op jit(solution)/shard_map/ppermute | solution.py:423
  148.3 0.0 collective-permute-done.1.far
  148.3 0.4 collective-permute-done.2.near
  148.6 3.7 %collective-permute-done.3.next_to = f32[128,256]{1,0:T(8,128)S(1)} collective-permute-done((f32[128,256]{1,0:T(8,128)S(1)}, f32[128,256]{1,0:T(8,128)S(1)}, u32[]{:S(2)}, u32[]{:S(2)}) %collective-permute-start.3) | collective-permute-done | bytes 131104 | tf_op jit(solution)/shard_map/ppermute | solution.py:423
  152.3 2.4 %all-to-all-done.8.blocks = f32[64,8,128]{2,1,0:T(8,128)S(1)} async-done(((f32[64,8,128]{2,1,0:T(8,128)}), f32[64,8,128]{2,1,0:T(8,128)S(1)}, u32[]{:S(2)}, u32[]{:S(2)}) %all-to-all-start.8) | async-done | bytes 262176 | tf_op jit(solution)/shard_map/all_to_all | solution.py:416
  154.8 0.8 last.1
  (7 shorter events, 0.2 us)
Async XLA Ops:
  115.6 9.2 %copy-start = (f32[2048,128]{1,0:T(8,128)S(1)}, f32[2048,128]{1,0:T(8,128)}, u32[]{:S(2)}) copy-start(f32[2048,128]{1,0:T(8,128)} %emb.3) | copy-start | bytes 3145732
  115.6 9.2 %copy-start.1 = (f32[512,128]{1,0:T(8,128)S(1)}, f32[512,128]{1,0:T(8,128)}, u32[]{:S(2)}) copy-start(f32[512,128]{1,0:T(8,128)} %proto.3) | copy-start | bytes 786436
  127.6 27.2 %all-to-all-start.8 = ((f32[64,8,128]{2,1,0:T(8,128)}), f32[64,8,128]{2,1,0:T(8,128)S(1)}, u32[]{:S(2)}, u32[]{:S(2)}) async-start(f32[64,8,128]{2,1,0:T(8,128)} %bitcast.15), calls=%async_computation.8 | async-start | bytes 524288 | tf_op jit(solution)/shard_map/all_to_all | solution.py:416
  134.0 3.8 %collective-permute-start = (f32[4,128,256]{2,1,0:T(8,128)S(1)}, f32[4,128,256]{2,1,0:T(8,128)S(1)}, u32[]{:S(2)}, u32[]{:S(2)}) collective-permute-start(f32[4,128,256]{2,1,0:T(8,128)S(1)} %get-tuple-element.44), channel_id=1, source_target_pairs={{0,64},{64,0},{1,65},{65,1},{2,66},{66,2},{3,67},{67,3},{4,68},{68... | collective-permute-start | bytes 1572872 | tf_op jit(solution)/shard_map/ppermute | solution.py:414
  138.4 9.8 %collective-permute-start.1 = (f32[128,256]{1,0:T(8,128)S(1)}, f32[128,256]{1,0:T(8,128)S(1)}, u32[]{:S(2)}, u32[]{:S(2)}) collective-permute-start(f32[128,256]{1,0:T(8,128)S(1)} %get-tuple-element.45), channel_id=1, source_target_pairs={{0,256},{128,384},{256,0},{384,128},{1,257},{129,385},{257,1},{385... | collective-permute-start | bytes 393224 | tf_op jit(solution)/shard_map/ppermute | solution.py:423
  141.3 7.3 %collective-permute-start.2 = (f32[128,256]{1,0:T(8,128)S(1)}, f32[128,256]{1,0:T(8,128)S(1)}, u32[]{:S(2)}, u32[]{:S(2)}) collective-permute-start(f32[128,256]{1,0:T(8,128)S(1)} %get-tuple-element.46), channel_id=1, source_target_pairs={{0,128},{128,0},{256,384},{384,256},{1,129},{129,1},{257,385},{385... | collective-permute-start | bytes 393224 | tf_op jit(solution)/shard_map/ppermute | solution.py:423
  144.3 8.1 %collective-permute-start.3 = (f32[128,256]{1,0:T(8,128)S(1)}, f32[128,256]{1,0:T(8,128)S(1)}, u32[]{:S(2)}, u32[]{:S(2)}) collective-permute-start(f32[128,256]{1,0:T(8,128)S(1)} %get-tuple-element.47), channel_id=1, source_target_pairs={{0,384},{128,256},{256,128},{384,0},{1,385},{129,257},{257,129},{3... | collective-permute-start | bytes 393224 | tf_op jit(solution)/shard_map/ppermute | solution.py:423

commit v7 on v6

--- a/solution.py
+++ b/solution.py
@@ -382,7 +382,7 @@
     )
     here, place = lax.optimization_barrier((here, place))
     f1, here = call(
-        col_kernel, "col_lse", [row, col], [(8, rows), tall, tall], [logits, to_all(here, comm)]
+        col_kernel, "col_lse", [row, col], [(8, rows), tall, tall], [logits, to_all(here, ("core", "y"))]
     )
     g1, here = call(
         lambda *refs: row_kernel(log_mass, *refs), "row_lse", [col, row], [tall],
@@ -390,7 +390,7 @@
     )
     f2, here = call(
         col_mean_kernel, "col_lse_mean", [row, two],
-        [(16, rows), tall, tall, tall], [logits, to_all(here, comm), grads],
+        [(16, rows), tall, tall, tall], [logits, to_all(here, ("core", "y")), grads],
     )
     (here,) = call(merge_kernel, "merge_x", [two], [], [to_all(here, "x")])
     score, here = call(
@@ -399,7 +399,7 @@
     )
     score, here = call(
         dg1_kernel, "dg1", [full, col], [(8, rows), (8, rows), tall, tall],
-        [logits, f2, g1, to_all(here, comm), score],
+        [logits, f2, g1, to_all(here, ("core", "y")), score],
     )
     score, here = call(
         lambda *refs: df1_kernel(log_mass, *refs), "df1", [full, row], [tall, tall],
@@ -408,7 +408,7 @@
     keep, send, proto_part = call(
         grads_kernel, "grads", [blocks, blocks, by_node],
         [by_node[0], pltpu.SemaphoreType.DMA],
-        [place, logits, f1, to_all(here, comm), score, embeddings, prototypes],
+        [place, logits, f1, to_all(here, ("core", "y")), score, embeddings, prototypes],
         {0: pltpu.SMEM}, {2: hbm},
     )
     other = lax.ppermute(send, "core", [(0, 1), (1, 0)])

time: 156 us -> 156 us (level)
  no operation moved by 1% of the time
where the time goes in v7:
time: 156 us
  blocking collectives  112 us (72%)
  starting transfers between devices  18.1 us (12%)
  Pallas kernels  15.2 us (10%)
  waiting for transfers between devices  8.68 us (6%)
    all_to_all x8, blocking collectives, to_all(): return lax.all_to_all(copies, axis, 0, 0, tiled=True)  112 us
    pallas_call x11, Pallas kernels, call(): pl.pallas_call(kernel, name=name, out_shape=[dict(out_places)[k](shape, d...  15.2 us
    ppermute x3, starting transfers between devices, on_device(): lax.ppermute(part, 'y', [(y, y ^ k) for y in range(ys)])  9.82 us
    all_to_all x1, starting transfers between devices, on_device(): proto_part = lax.all_to_all(proto_part, ('x', 'z'), 0, 0, tiled=True)  6.4 us
    ppermute x3, waiting for transfers between devices, on_device(): lax.ppermute(part, 'y', [(y, y ^ k) for y in range(ys)])  4.35 us
  transfers between devices with their start and end apart: 5, of which 4 were waited for; matrix products, arithmetic and copies ran while one was open for 0% of the time, Pallas kernels for 0%

profile of v7, /device:TPU:6, one launch (start us, length us, event | category | flops | bytes accessed | tf_op | source)
XLA Modules:
  0.0 155.7 jit_solution(15716242526045164652)
XLA Ops:
  0.6 0.1 pad_add_fusion.place.refs_0_
  0.7 4.2 %scores.1 = (f32[512,2048]{1,0:T(8,128)S(1)}, bf16[512,2048]{1,0:T(8,128)(2,1)S(1)}, f32[1,2048]{1,0:T(1,128)S(1)}) custom-call(f32[2048,128]{1,0:T(8,128)} %emb.3, f32[512,128]{1,0:T(8,128)} %proto.3, bf16[2048,512]{1,0:T(8,128)(2,1)} %grads.2), custom_call_target="tpu_custom_call" | custom-call | tf_op jit(solution)/shard_map/scores/pallas_call | solution.py:335
  5.0 9.6 %all_to_all.45.parts = f32[8,1,2048]{2,1,0:T(1,128)S(1)} all-to-all(f32[8,1,2048]{2,1,0:T(1,128)S(1)} %broadcast_in_dim.29), channel_id=1, replica_groups=mesh['y'=4,'core'=2,'z'=16,'x'=4] {'core','y'}, dimensions={0} | all-to-all | bytes 131072 | tf_op jit(solution)/shard_map/all_to_all | solution.py:25
  14.6 1.0 col_lse.1
  15.6 0.1 broadcast_in_dim.31
  15.7 34.4 %all_to_all.46.refs_1_ = f32[64,1,512]{2,1,0:T(1,128)S(1)} all-to-all(f32[64,1,512]{2,1,0:T(1,128)S(1)} %broadcast_in_dim.31), channel_id=1, replica_groups=mesh['y'=4,'core'=2,'z'=16,'x'=4] {'x','z'}, dimensions={0} | all-to-all | bytes 262144 | tf_op jit(solution)/shard_map/all_to_all | solution.py:25
  50.1 1.1 row_lse.1
  51.2 7.7 %all_to_all.47.parts = f32[8,1,2048]{2,1,0:T(1,128)S(1)} all-to-all(f32[8,1,2048]{2,1,0:T(1,128)S(1)} %broadcast_in_dim.65), channel_id=1, replica_groups=mesh['y'=4,'core'=2,'z'=16,'x'=4] {'core','y'}, dimensions={0} | all-to-all | bytes 131072 | tf_op jit(solution)/shard_map/all_to_all | solution.py:25
  58.9 1.4 col_lse_mean.1
  60.3 7.8 %all_to_all.48.parts = f32[4,2,512]{2,1,0:T(2,128)S(1)} all-to-all(f32[4,2,512]{2,1,0:T(2,128)S(1)} %broadcast_in_dim.66), channel_id=1, replica_groups=mesh['y'=4,'core'=2,'z'=16,'x'=4] {'x'}, dimensions={0} | all-to-all | bytes 32768 | tf_op jit(solution)/shard_map/all_to_all | solution.py:25
  68.2 15.5 %all_to_all.49.refs_2_ = f32[16,2,512]{2,1,0:T(2,128)S(1)} all-to-all(f32[16,2,512]{2,1,0:T(2,128)S(1)} %broadcast_in_dim.67), channel_id=1, replica_groups=mesh['y'=4,'core'=2,'z'=16,'x'=4] {'z'}, dimensions={0} | all-to-all | bytes 131072 | tf_op jit(solution)/shard_map/all_to_all | solution.py:25
  83.7 1.2 df2.1
  84.9 7.9 %all_to_all.50.parts = f32[8,1,2048]{2,1,0:T(1,128)S(1)} all-to-all(f32[8,1,2048]{2,1,0:T(1,128)S(1)} %broadcast_in_dim.69), channel_id=1, replica_groups=mesh['y'=4,'core'=2,'z'=16,'x'=4] {'core','y'}, dimensions={0} | all-to-all | bytes 131072 | tf_op jit(solution)/shard_map/all_to_all | solution.py:25
  92.8 1.0 dg1.1
  93.8 0.1 broadcast_in_dim.71
  93.9 21.8 %all_to_all.51.refs_3_ = f32[64,1,512]{2,1,0:T(1,128)S(1)} all-to-all(f32[64,1,512]{2,1,0:T(1,128)S(1)} %broadcast_in_dim.71), channel_id=1, replica_groups=mesh['y'=4,'core'=2,'z'=16,'x'=4] {'x','z'}, dimensions={0} | all-to-all | bytes 262144 | tf_op jit(solution)/shard_map/all_to_all | solution.py:25
  115.7 0.0 copy-start
  115.7 0.0 copy-start.1
  115.7 1.1 df1.1
  116.9 7.7 %all_to_all.52.parts = f32[8,1,2048]{2,1,0:T(1,128)S(1)} all-to-all(f32[8,1,2048]{2,1,0:T(1,128)S(1)} %broadcast_in_dim.73), channel_id=1, replica_groups=mesh['y'=4,'core'=2,'z'=16,'x'=4] {'core','y'}, dimensions={0} | all-to-all | bytes 131072 | tf_op jit(solution)/shard_map/all_to_all | solution.py:25
  124.6 0.0 copy-done
  124.6 0.0 copy-done.1
  124.6 2.8 %grads.3 = (f32[4,128,256]{2,1,0:T(8,128)S(1)}, f32[4,128,256]{2,1,0:T(8,128)S(1)}, f32[4,16,8,128]{3,2,1,0:T(8,128)}) custom-call(s32[2]{0:T(128)S(1)} %pad_add_fusion.place.refs_0_, f32[512,2048]{1,0:T(8,128)S(1)} %get-tuple-element.28.logits.refs_0_, f32[1,2048]{1,0:T(1,128)S(1)} %get-tuple-element.30.refs_1_.f1, f32[8,1,2048]{2,1,0:T(1,128)S(1)} %all_to_all.52.parts, ...), custom_call_target="tpu_custom_call" | custom-call | tf_op jit(solution)/shard_map/grads/pallas_call | solution.py:335
  127.4 6.4 %all-to-all-start.8 = ((f32[64,8,128]{2,1,0:T(8,128)}), f32[64,8,128]{2,1,0:T(8,128)S(1)}, u32[]{:S(2)}, u32[]{:S(2)}) async-start(f32[64,8,128]{2,1,0:T(8,128)} %bitcast.15), calls=%async_computation.8 | async-start | bytes 524288 | tf_op jit(solution)/shard_map/all_to_all | solution.py:416
  133.8 1.9 %collective-permute-start = (f32[4,128,256]{2,1,0:T(8,128)S(1)}, f32[4,128,256]{2,1,0:T(8,128)S(1)}, u32[]{:S(2)}, u32[]{:S(2)}) collective-permute-start(f32[4,128,256]{2,1,0:T(8,128)S(1)} %get-tuple-element.44), channel_id=1, source_target_pairs={{0,64},{64,0},{1,65},{65,1},{2,66},{66,2},{3,67},{67,3},{4,68},{68... | collective-permute-start | bytes 1572872 | tf_op jit(solution)/shard_map/ppermute | solution.py:414
  135.7 1.9 %collective-permute-done.refs_2_ = f32[4,128,256]{2,1,0:T(8,128)S(1)} collective-permute-done((f32[4,128,256]{2,1,0:T(8,128)S(1)}, f32[4,128,256]{2,1,0:T(8,128)S(1)}, u32[]{:S(2)}, u32[]{:S(2)}) %collective-permute-start) | collective-permute-done | bytes 524320 | tf_op jit(solution)/shard_map/ppermute | solution.py:414
  137.6 0.6 emb_pair.1
  138.2 3.1 %collective-permute-start.1 = (f32[128,256]{1,0:T(8,128)S(1)}, f32[128,256]{1,0:T(8,128)S(1)}, u32[]{:S(2)}, u32[]{:S(2)}) collective-permute-start(f32[128,256]{1,0:T(8,128)S(1)} %get-tuple-element.45), channel_id=1, source_target_pairs={{0,256},{128,384},{256,0},{384,128},{1,257},{129,385},{257,1},{385... | collective-permute-start | bytes 393224 | tf_op jit(solution)/shard_map/ppermute | solution.py:423
  141.3 3.0 %collective-permute-start.2 = (f32[128,256]{1,0:T(8,128)S(1)}, f32[128,256]{1,0:T(8,128)S(1)}, u32[]{:S(2)}, u32[]{:S(2)}) collective-permute-start(f32[128,256]{1,0:T(8,128)S(1)} %get-tuple-element.46), channel_id=1, source_target_pairs={{0,128},{128,0},{256,384},{384,256},{1,129},{129,1},{257,385},{385... | collective-permute-start | bytes 393224 | tf_op jit(solution)/shard_map/ppermute | solution.py:423
  144.4 3.7 %collective-permute-start.3 = (f32[128,256]{1,0:T(8,128)S(1)}, f32[128,256]{1,0:T(8,128)S(1)}, u32[]{:S(2)}, u32[]{:S(2)}) collective-permute-start(f32[128,256]{1,0:T(8,128)S(1)} %get-tuple-element.47), channel_id=1, source_target_pairs={{0,384},{128,256},{256,128},{384,0},{1,385},{129,257},{257,129},{3... | collective-permute-start | bytes 393224 | tf_op jit(solution)/shard_map/ppermute | solution.py:423
  148.1 0.0 collective-permute-done.1.far
  148.1 0.7 collective-permute-done.2.near
  148.7 3.7 %collective-permute-done.3.next_to = f32[128,256]{1,0:T(8,128)S(1)} collective-permute-done((f32[128,256]{1,0:T(8,128)S(1)}, f32[128,256]{1,0:T(8,128)S(1)}, u32[]{:S(2)}, u32[]{:S(2)}) %collective-permute-start.3) | collective-permute-done | bytes 131104 | tf_op jit(solution)/shard_map/ppermute | solution.py:423
  152.4 2.5 %all-to-all-done.8.blocks = f32[64,8,128]{2,1,0:T(8,128)S(1)} async-done(((f32[64,8,128]{2,1,0:T(8,128)}), f32[64,8,128]{2,1,0:T(8,128)S(1)}, u32[]{:S(2)}, u32[]{:S(2)}) %all-to-all-start.8) | async-done | bytes 262176 | tf_op jit(solution)/shard_map/all_to_all | solution.py:416
  154.9 0.8 last.1
  (7 shorter events, 0.2 us)
Async XLA Ops:
  115.7 8.9 %copy-start = (f32[2048,128]{1,0:T(8,128)S(1)}, f32[2048,128]{1,0:T(8,128)}, u32[]{:S(2)}) copy-start(f32[2048,128]{1,0:T(8,128)} %emb.3) | copy-start | bytes 3145732
  115.7 8.9 %copy-start.1 = (f32[512,128]{1,0:T(8,128)S(1)}, f32[512,128]{1,0:T(8,128)}, u32[]{:S(2)}) copy-start(f32[512,128]{1,0:T(8,128)} %proto.3) | copy-start | bytes 786436
  127.4 27.5 %all-to-all-start.8 = ((f32[64,8,128]{2,1,0:T(8,128)}), f32[64,8,128]{2,1,0:T(8,128)S(1)}, u32[]{:S(2)}, u32[]{:S(2)}) async-start(f32[64,8,128]{2,1,0:T(8,128)} %bitcast.15), calls=%async_computation.8 | async-start | bytes 524288 | tf_op jit(solution)/shard_map/all_to_all | solution.py:416
  133.8 3.8 %collective-permute-start = (f32[4,128,256]{2,1,0:T(8,128)S(1)}, f32[4,128,256]{2,1,0:T(8,128)S(1)}, u32[]{:S(2)}, u32[]{:S(2)}) collective-permute-start(f32[4,128,256]{2,1,0:T(8,128)S(1)} %get-tuple-element.44), channel_id=1, source_target_pairs={{0,64},{64,0},{1,65},{65,1},{2,66},{66,2},{3,67},{67,3},{4,68},{68... | collective-permute-start | bytes 1572872 | tf_op jit(solution)/shard_map/ppermute | solution.py:414
  138.2 9.8 %collective-permute-start.1 = (f32[128,256]{1,0:T(8,128)S(1)}, f32[128,256]{1,0:T(8,128)S(1)}, u32[]{:S(2)}, u32[]{:S(2)}) collective-permute-start(f32[128,256]{1,0:T(8,128)S(1)} %get-tuple-element.45), channel_id=1, source_target_pairs={{0,256},{128,384},{256,0},{384,128},{1,257},{129,385},{257,1},{385... | collective-permute-start | bytes 393224 | tf_op jit(solution)/shard_map/ppermute | solution.py:423
  141.3 7.4 %collective-permute-start.2 = (f32[128,256]{1,0:T(8,128)S(1)}, f32[128,256]{1,0:T(8,128)S(1)}, u32[]{:S(2)}, u32[]{:S(2)}) collective-permute-start(f32[128,256]{1,0:T(8,128)S(1)} %get-tuple-element.46), channel_id=1, source_target_pairs={{0,128},{128,0},{256,384},{384,256},{1,129},{129,1},{257,385},{385... | collective-permute-start | bytes 393224 | tf_op jit(solution)/shard_map/ppermute | solution.py:423
  144.4 8.1 %collective-permute-start.3 = (f32[128,256]{1,0:T(8,128)S(1)}, f32[128,256]{1,0:T(8,128)S(1)}, u32[]{:S(2)}, u32[]{:S(2)}) collective-permute-start(f32[128,256]{1,0:T(8,128)S(1)} %get-tuple-element.47), channel_id=1, source_target_pairs={{0,384},{128,256},{256,128},{384,0},{1,385},{129,257},{257,129},{3... | collective-permute-start | bytes 393224 | tf_op jit(solution)/shard_map/ppermute | solution.py:423
